TPU v7x, 32 devices: a whole 2x2x4 slice. The times are simulated.
32 devices in a mesh: node: 8 (over z, core), feat: 4 (over y, x).
Axes of the slice: x: 2, y: 2, z: 4, core: 2. Of those that a mesh axis runs over, the one named last changes fastest.
Arguments:
- x_feat: bfloat16 [512, 32768], P('feat', 'node'), may hold values from -6 to 6
- weight: bfloat16 [512, 512], P('feat'), may hold values from -1 to 1
- out_grad: bfloat16 [512, 32768], P('feat', 'node'), may hold values from -12 to 12
- tile_rows: int32 [960], P('node'), may hold values from 0 to 31, as said below
- tile_cols: int32 [960], P('node'), may hold values from 0 to 255, as said below
- tile_masks: int32 [960, 128, 128], P('node'), may hold values from 0 to 1
Outputs:
- activ: bfloat16 [512, 32768], P('feat', 'node')
- x_grad: bfloat16 [512, 32768], P('feat', 'node')
- weight_grad: float32 [512, 512], P('feat')
Inputs may be any that keep to these rules, and one draw needn't show every extreme that they name: `tile_rows`: each node shard's first 32 tiles are its row blocks 0 to 31 in order, each with its own block as column block. `tile_cols`: the tiles of one node shard read at most 8 distinct column blocks held by any one other node shard; in every draw some node shard reads exactly 8 blocks of some other.
All inputs are finite; a program needn't handle non-finite values.
Results may differ from a plain program's by a relative error of at most 0.013.
Values may be sent and summed in bfloat16 or wider, within the bound.
A program may use at most 128 MiB of HBM per device.

v0:
```python
import jax
import jax.numpy as jnp
from jax import lax
from jax.sharding import PartitionSpec as P

exact_precision = lax.Precision.HIGHEST


def silu_slope(value):
    sig = jax.nn.sigmoid(value)
    return sig * (1.0 + value * (1.0 - sig))


def per_device(x_feat, weight, out_grad, tile_rows, tile_cols, tile_masks):
    shards = lax.axis_size("node")
    block = tile_masks.shape[1]
    feat_dev = x_feat.shape[0]
    local_rows = x_feat.shape[1]
    local_blocks = local_rows // block
    all_blocks = local_blocks * shards
    nodes_total = local_rows * shards
    edge_values = tile_masks.astype(jnp.bfloat16)
    row_onehot = (tile_rows[None, :] == jnp.arange(local_blocks, dtype=jnp.int32)[:, None]).astype(
        jnp.float32
    )
    degree = 1.0 + jnp.dot(
        row_onehot, jnp.sum(tile_masks, axis=2).astype(jnp.float32), precision=exact_precision
    )
    x_blocks = x_feat.reshape(feat_dev, local_blocks, block)
    gathered = lax.all_gather(x_feat, "node", axis=1, tiled=True)
    source = jnp.take(gathered.reshape(feat_dev, all_blocks, block), tile_cols, axis=1)
    tile_terms = jnp.einsum("ftc,trc->ftr", source, edge_values, preferred_element_type=jnp.float32)
    summed = jnp.einsum("bt,ftr->fbr", row_onehot, tile_terms, precision=exact_precision)
    aggregated = (
        ((x_blocks.astype(jnp.float32) + summed) / degree[None])
        .astype(jnp.bfloat16)
        .reshape(feat_dev, local_rows)
    )
    node_rows = lax.all_to_all(aggregated, "feat", split_axis=1, concat_axis=0, tiled=True)
    full_weight = lax.all_gather(weight, "feat", axis=0, tiled=True)
    row_preact = lax.dot_general(
        full_weight, node_rows, (((0,), (0,)), ((), ())), preferred_element_type=jnp.float32
    )
    row_activ = jax.nn.silu(row_preact).astype(jnp.bfloat16)
    activ = lax.all_to_all(row_activ, "feat", split_axis=0, concat_axis=1, tiled=True)
    cotangent_rows = lax.all_to_all(out_grad, "feat", split_axis=1, concat_axis=0, tiled=True)
    grad_rows = (cotangent_rows.astype(jnp.float32) * silu_slope(row_preact)).astype(jnp.bfloat16)
    row_hidden = jnp.dot(full_weight, grad_rows, preferred_element_type=jnp.float32).astype(
        jnp.bfloat16
    )
    hidden_grad = lax.all_to_all(row_hidden, "feat", split_axis=0, concat_axis=1, tiled=True)
    full_part = lax.dot_general(
        node_rows, grad_rows, (((1,), (1,)), ((), ())), preferred_element_type=jnp.float32
    )
    part_grad = lax.psum_scatter(full_part, "feat", scatter_dimension=0, tiled=True)
    weight_grad = lax.psum(part_grad, "node") * nodes_total ** (-0.5)
    scaled = (
        hidden_grad.reshape(feat_dev, local_blocks, block).astype(jnp.float32) / degree[None]
    ).astype(jnp.bfloat16)
    row_source = jnp.take(scaled, tile_rows, axis=1)
    contrib = jnp.einsum(
        "ftr,trc->ftc", row_source, edge_values, preferred_element_type=jnp.float32
    )
    col_hits = (tile_cols[None, :] == jnp.arange(all_blocks, dtype=jnp.int32)[:, None]).astype(
        jnp.float32
    )
    spread = jnp.einsum("st,ftc->fsc", col_hits, contrib, precision=exact_precision)
    returned = lax.psum_scatter(
        spread.astype(jnp.bfloat16), "node", scatter_dimension=1, tiled=True
    ).astype(jnp.float32)
    x_grad = (
        (scaled.astype(jnp.float32) + returned).astype(jnp.bfloat16).reshape(feat_dev, local_rows)
    )
    return (activ, x_grad, weight_grad)


def solution(mesh):
    placed = (
        P("feat", "node"),
        P("feat", None),
        P("feat", "node"),
        P("node"),
        P("node"),
        P("node", None, None),
    )
    return jax.shard_map(
        per_device,
        mesh=mesh,
        in_specs=placed,
        out_specs=(P("feat", "node"), P("feat", "node"), P("feat", None)),
        check_vma=False,
    )
```

profile of v0, /device:TPU:0, one launch (start us, length us, event | category | flops | bytes accessed | tf_op | source)
XLA Modules:
  0.0 350.5 jit_solution(9914526656599863698)
XLA Ops:
  7.2 0.0 all-gather.2.cloned.1.call-start
  7.2 2.3 copy.29
  9.6 0.0 all-gather.2.cloned.1.call-update
  9.6 2.3 copy.55
  11.9 5.2 %all-to-all-start.2 = ((bf16[128,4,1024]{2,0,1:T(8,128)(2,1)}), bf16[128,4,1024]{2,0,1:T(8,128)(2,1)}, u32[]{:S(2)}, u32[]{:S(2)}) async-start(bf16[128,4,1024]{2,0,1:T(8,128)(2,1)} %bitcast.86), calls=%async_computation.2 | async-start | bytes 2097152 | tf_op jit(solution)/shard_map/all_to_all | solution.py:46
  17.0 0.2 convert_bitcast_fusion.2
  17.2 0.4 copy.42
  17.6 0.0 copy-start.4
  17.6 0.0 copy-start.3
  17.6 5.9 %reduce_sum.9 = s32[120,128]{1,0:T(8,128)S(1)} reduce(s32[120,128,128]{2,1,0:T(8,128)} %param.11, s32[]{:T(128)} %constant.20.clone.1), dimensions={2}, to_apply=%region_0.0 | reduce | flops 1950720 | bytes 7925764 | tf_op jit(solution)/shard_map/reduce_sum | solution.py:27
  23.6 0.1 convolution_add_fusion
  23.7 71.3 %all-gather.2.cloned.1.call-done = bf16[128,32768]{0,1:T(8,128)(2,1)} async-done(((bf16[128,4096]{0,1:T(8,128)(2,1)}), bf16[128,32768]{0,1:T(8,128)(2,1)}) %all-gather.2.cloned.1.call-update) | async-done | bytes 8388624 | tf_op jit(solution)/shard_map/all_gather | solution.py:30
  95.0 11.9 %copy.30 = bf16[128,256,128]{2,0,1:T(8,128)(2,1)} copy(bf16[128,256,128]{0,2,1:T(8,128)(2,1)} %bitcast.87) | data formatting | bytes 16777216 | tf_op jit(solution)/shard_map/reshape | solution.py:31
  106.9 6.3 %gather_fusion = bf16[120,128,128]{2,1,0:T(8,128)(2,1)} fusion(bf16[128,256,128]{2,0,1:T(8,128)(2,1)} %copy.30, s32[1024]{0:T(1024)S(1)} %pad_clamp_fusion.1), kind=kCustom, calls=%fused_computation | custom fusion | bytes 7864800 | tf_op jit(solution)/shard_map/jit(_take)/gather | solution.py:31
  113.2 7.3 %fusion.14 = f32[128,120,128]{2,0,1:T(8,128)S(1)} fusion(bf16[120,128,128]{2,1,0:T(8,128)(2,1)} %gather_fusion, pred[120]{0:T(512)(128)(4,1)S(1)} %compare_and_fusion.1, s32[120,128,128]{2,1,0:T(8,128)} %param.11), kind=kOutput, calls=%fused_computation.15 | convolution fusion | flops 507248640 | bytes 19660920 | tf_op jit(solution)/shard_map/ftc,trc->ftr/dot_general | solution.py:32
  120.5 7.7 %fusion.21 = bf16[128,32,128]{2,1,0:T(8,128)(2,1)S(1)} fusion(f32[16,8,32,128]{3,2,1,0:T(8,128)S(1)} %copy.42, f32[128,120,128]{2,0,1:T(8,128)S(1)} %fusion.14, f32[32,128]{1,0:T(8,128)S(1)} %convolution_add_fusion, s32[120]{0:T(128)S(1)} %copy-done.3), kind=kOutput, calls=%fused_computation.19 | convolution fusion | flops 756551424 | bytes 11026912 | tf_op jit(solution)/shard_map/bt,ftr->fbr/dot_general | solution.py:33
  128.2 0.0 copy-start.2
  128.2 0.3 all_to_all.48
  128.5 1.3 copy.32
  129.8 3.7 %all-to-all-start = ((bf16[128,4,1024]{2,0,1:T(8,128)(2,1)}), bf16[128,4,1024]{2,0,1:T(8,128)(2,1)S(1)}, u32[]{:S(2)}, u32[]{:S(2)}) async-start(bf16[128,4,1024]{2,0,1:T(8,128)(2,1)} %copy.32), calls=%async_computation | async-start | bytes 2097152 | tf_op jit(solution)/shard_map/all_to_all | solution.py:39
  133.5 19.9 %all_gather.7 = bf16[512,512]{1,0:T(8,128)(2,1)S(1)} all-gather(bf16[128,512]{1,0:T(8,128)(2,1)S(1)} %copy-done.2), channel_id=1, replica_groups=mesh['node'=8,'feat'=4] {'feat'}, dimensions={0}, use_global_device_ids=true | all-gather | bytes 655360 | tf_op jit(solution)/shard_map/all_gather | solution.py:40
  153.4 3.6 %fusion.22 = (bf16[512,1024]{1,0:T(8,128)(2,1)S(1)}, bf16[512,1024]{1,0:T(8,128)(2,1)}) fusion(bf16[128,4,1024]{2,0,1:T(8,128)(2,1)} %all-to-all-done.2, bf16[512,1024]{1,0:T(8,128)(2,1)S(1)} %bitcast.92, bf16[512,512]{1,0:T(8,128)(2,1)S(1)} %all_gather.7), kind=kOutput, calls=%fused_computation.21 | convolution fusion | flops 543162368 | bytes 4718592 | tf_op jit(solution)/shard_map/dot_general | solution.py:41
  157.1 1.7 convolution_convert_fusion
  158.8 3.5 %all-to-all-start.3 = ((bf16[4,128,1024]{2,1,0:T(8,128)(2,1)}), bf16[4,128,1024]{2,1,0:T(8,128)(2,1)S(1)}, u32[]{:S(2)}, u32[]{:S(2)}) async-start(bf16[4,128,1024]{2,1,0:T(8,128)(2,1)} %bitcast.13), calls=%async_computation.3 | async-start | bytes 2097152 | tf_op jit(solution)/shard_map/all_to_all | solution.py:51
  162.3 0.0 reduce-scatter.5.cloned.1.call-start
  162.3 1.7 fusion.45
  164.1 0.0 reduce-scatter.5.cloned.1.call-update
  164.1 0.0 all-reduce.2.cloned.1.call-start
  164.2 12.5 %all-to-all-done.3 = bf16[4,128,1024]{2,1,0:T(8,128)(2,1)S(1)} async-done(((bf16[4,128,1024]{2,1,0:T(8,128)(2,1)}), bf16[4,128,1024]{2,1,0:T(8,128)(2,1)S(1)}, u32[]{:S(2)}, u32[]{:S(2)}) %all-to-all-start.3) | async-done | bytes 1048608 | tf_op jit(solution)/shard_map/all_to_all | solution.py:51
  176.7 0.2 convert_bitcast_fusion.1
  176.9 2.7 copy.35
  179.6 2.1 reshape.52
  181.7 0.2 divide_convert_fusion
  181.9 0.4 copy.36
  182.3 2.9 gather_fusion.1
  185.3 8.9 %fusion.17 = f32[128,120,128]{2,0,1:T(8,128)} fusion(bf16[120,128,128]{2,1,0:T(8,128)(2,1)} %gather_fusion.1, pred[120]{0:T(512)(128)(4,1)S(1)} %compare_and_fusion, s32[120,128,128]{2,1,0:T(8,128)} %param.11), kind=kOutput, calls=%fused_computation.16 | convolution fusion | flops 507248640 | bytes 19660920 | tf_op jit(solution)/shard_map/ftr,trc->ftc/dot_general | solution.py:61
  194.2 0.0 all-reduce.2.cloned.1.call-update
  194.2 0.3 reduce-scatter.3.cloned.1.call-start
  194.5 23.6 %convert_bitcast_fusion = bf16[128,256,128]{2,1,0:T(8,128)(2,1)} fusion(f32[128,120,128]{2,0,1:T(8,128)} %fusion.17, s32[120]{0:T(128)S(1)} %copy-done.4), kind=kOutput, calls=%fused_computation.2 | convolution fusion | flops 6044022784 | bytes 16253408 | tf_op jit(solution)/shard_map/st,ftc->fsc/dot_general | solution.py:67
  218.1 0.0 reduce-scatter.3.cloned.1.call-update
  218.1 1.2 copy-done.1
  219.3 15.4 %all_to_all.64 = bf16[4,128,1024]{2,1,0:T(8,128)(2,1)S(1)} all-to-all(bf16[4,128,1024]{2,1,0:T(8,128)(2,1)S(1)} %bitcast.91), channel_id=1, replica_groups=mesh['node'=8,'feat'=4] {'feat'}, dimensions={0} | all-to-all | bytes 2097152 | tf_op jit(solution)/shard_map/all_to_all | solution.py:45
  234.8 1.1 copy.41
  235.8 14.4 %all-reduce.2.cloned.1.call-done = f32[128,512]{1,0:T(8,128)} async-done(((f32[128,512]{1,0:T(8,128)}), f32[128,512]{1,0:T(8,128)}) %all-reduce.2.cloned.1.call-update) | async-done | bytes 262160 | tf_op jit(solution)/shard_map/psum | solution.py:56
  250.2 1.7 broadcast_multiply_fusion
  251.9 89.1 %reduce-scatter.3.cloned.1.call-done = bf16[128,32,128]{2,1,0:T(8,128)(2,1)} async-done(((bf16[128,256,128]{2,1,0:T(8,128)(2,1)}), bf16[128,32,128]{2,1,0:T(8,128)(2,1)}) %reduce-scatter.3.cloned.1.call-update) | async-done | bytes 1048592 | tf_op jit(solution)/shard_map/reduce_scatter | solution.py:68
  341.0 1.6 add_convert_fusion
  342.6 1.4 copy.54
  (15 shorter events, 0.1 us)
Async XLA Ops:
  7.2 9.9 %copy-start = (bf16[128,4096]{1,0:T(8,128)(2,1)S(1)}, bf16[128,4096]{1,0:T(8,128)(2,1)}, u32[]{:S(2)}) copy-start(bf16[128,4096]{1,0:T(8,128)(2,1)} %param.6) | copy-start | bytes 3145732
  7.2 87.8 %all-gather.2.cloned.1.call-start = ((), (), s32[]{:S(2)}) async-start(), calls=%async_computation.6 | async-start | bytes 9437184 | tf_op jit(solution)/shard_map/all_gather | solution.py:30
  11.9 117.9 %all-to-all-start.2 = ((bf16[128,4,1024]{2,0,1:T(8,128)(2,1)}), bf16[128,4,1024]{2,0,1:T(8,128)(2,1)}, u32[]{:S(2)}, u32[]{:S(2)}) async-start(bf16[128,4,1024]{2,0,1:T(8,128)(2,1)} %bitcast.86), calls=%async_computation.2 | async-start | bytes 2097152 | tf_op jit(solution)/shard_map/all_to_all | solution.py:46
  17.6 5.9 %copy-start.4 = (s32[120]{0:T(128)S(1)}, s32[120]{0:T(128)}, u32[]{:S(2)}) copy-start(s32[120]{0:T(128)} %param.10) | copy-start | bytes 1444
  17.6 5.9 %copy-start.3 = (s32[120]{0:T(128)S(1)}, s32[120]{0:T(128)}, u32[]{:S(2)}) copy-start(s32[120]{0:T(128)} %param.9) | copy-start | bytes 1444
  128.2 5.3 %copy-start.2 = (bf16[128,512]{1,0:T(8,128)(2,1)S(1)}, bf16[128,512]{1,0:T(8,128)(2,1)}, u32[]{:S(2)}) copy-start(bf16[128,512]{1,0:T(8,128)(2,1)} %param.7) | copy-start | bytes 393220
  129.8 23.6 %all-to-all-start = ((bf16[128,4,1024]{2,0,1:T(8,128)(2,1)}), bf16[128,4,1024]{2,0,1:T(8,128)(2,1)S(1)}, u32[]{:S(2)}, u32[]{:S(2)}) async-start(bf16[128,4,1024]{2,0,1:T(8,128)(2,1)} %copy.32), calls=%async_computation | async-start | bytes 2097152 | tf_op jit(solution)/shard_map/all_to_all | solution.py:39
  158.8 17.9 %all-to-all-start.3 = ((bf16[4,128,1024]{2,1,0:T(8,128)(2,1)}), bf16[4,128,1024]{2,1,0:T(8,128)(2,1)S(1)}, u32[]{:S(2)}, u32[]{:S(2)}) async-start(bf16[4,128,1024]{2,1,0:T(8,128)(2,1)} %bitcast.13), calls=%async_computation.3 | async-start | bytes 2097152 | tf_op jit(solution)/shard_map/all_to_all | solution.py:51
  162.3 31.9 %reduce-scatter.5.cloned.1.call-start = ((), (), s32[]{:S(2)}) async-start(), calls=%async_computation.8 | async-start | bytes 1310720 | tf_op jit(solution)/shard_map/reduce_scatter | solution.py:55
  164.1 86.1 %all-reduce.2.cloned.1.call-start = ((), (), s32[]{:S(2)}) async-start(), calls=%async_computation.9 | async-start | bytes 524288 | tf_op jit(solution)/shard_map/psum | solution.py:56
  194.2 146.8 %reduce-scatter.3.cloned.1.call-start = ((), (), s32[]{:S(2)}) async-start(), calls=%async_computation.7 | async-start | bytes 9437184 | tf_op jit(solution)/shard_map/reduce_scatter | solution.py:68
  218.1 1.2 copy-start.1
Sparse Core Ops, SparseCore 0:
  10.2 84.7 all-gather.1
  166.0 26.7 reduce-scatter.4
  195.3 54.8 all-reduce.1
  252.4 88.5 reduce-scatter.2
where the time goes:
time: 351 us
  waiting for transfers between devices  187 us (53%)
  matrix products  54.7 us (16%)
  local copies, waits for them, and re-layouts  36.6 us (10%)
  blocking collectives  35.4 us (10%)
  between operations  14 us (4%)
  starting transfers between devices  12.8 us (4%)
  other arithmetic  9.81 us (3%)
    reduce_scatter x1, waiting for transfers between devices, per_device(): lax.psum_scatter(spread.astype(jnp.bfloat16), 'node', scatter_dimension=1...  89.1 us
    all_gather x1, waiting for transfers between devices, per_device(): gathered = lax.all_gather(x_feat, 'node', axis=1, tiled=True)  71.3 us
    dot_general x1, matrix products, per_device(): jnp.einsum('st,ftc->fsc', col_hits, contrib, precision=exact_precision)  23.6 us
    all_gather x1, blocking collectives, per_device(): full_weight = lax.all_gather(weight, 'feat', axis=0, tiled=True)  19.9 us
    all_to_all x1, blocking collectives, per_device(): lax.all_to_all(row_activ, 'feat', split_axis=0, concat_axis=1, tiled=True)  15.4 us
    psum x1, waiting for transfers between devices, per_device(): weight_grad = lax.psum(part_grad, 'node') * nodes_total ** (-0.5)  14.4 us
    all_to_all x1, waiting for transfers between devices, per_device(): lax.all_to_all(row_hidden, 'feat', split_axis=0, concat_axis=1, tiled=True)  12.5 us
    reshape x1, local copies, waits for them, and re-layouts, per_device(): gathered.reshape(feat_dev, all_blocks, block)  11.9 us
  transfers between devices with their start and end apart: 7, of which 4 were waited for; matrix products, arithmetic and copies ran while one was open for 25% of the time, Pallas kernels for 0%

commit v1 on v0

v1 whole, which is shorter than its diff:
```python
import functools

import jax
import jax.numpy as jnp
from jax import lax
from jax.experimental import pallas as pl
from jax.experimental.pallas import tpu as pltpu
from jax.sharding import PartitionSpec as P

CAP = 8
GROUP = 8
LANES = 128
MESH = pl.DeviceIdType.MESH
VMEM = pltpu.VMEM
SMEM = pltpu.SMEM
ANY = pl.ANY


def spec(space):
    return pl.BlockSpec(memory_space=space)


def params(limit_mib, **more):
    return pltpu.CompilerParams(vmem_limit_bytes=limit_mib << 20, **more)


def plan_kernel(shards, blocks, tiles, cols_ref, need_ref, slot_ref, pos, count):
    me = lax.axis_index("node")

    @pl.loop(0, shards)
    def _(s):
        count[s] = 0
        for k in range(CAP):
            need_ref[s, k] = 0

    @pl.loop(0, tiles)
    def _(t):
        pos[cols_ref[t]] = -1

    @pl.loop(0, tiles)
    def _(t):
        col = cols_ref[t]
        shard = col // blocks
        local = col - shard * blocks

        @pl.when(shard == me)
        def _():
            slot_ref[t] = local

        @pl.when(shard != me)
        def _():
            @pl.when(pos[col] < 0)
            def _():
                fresh = count[shard]
                pos[col] = fresh
                count[shard] = fresh + 1
                need_ref[shard, fresh] = local

            slot_ref[t] = blocks + shard * CAP + pos[col]


def barrier(shards, feats):
    node, feat = lax.axis_index("node"), lax.axis_index("feat")
    sem = pltpu.get_barrier_semaphore()
    for off in range(1, shards):
        pl.semaphore_signal(
            sem, inc=1, device_id=(lax.rem(node + off, shards), feat), device_id_type=MESH
        )
    for off in range(1, feats):
        pl.semaphore_signal(
            sem, inc=1, device_id=(node, lax.rem(feat + off, feats)), device_id_type=MESH
        )
    pl.semaphore_wait(sem, shards - 1 + (feats - 1 if feats else 0))


def ask_kernel(shards, need_ref, asked_ref, send_sem, recv_sem, self_sem):
    node, feat = lax.axis_index("node"), lax.axis_index("feat")
    barrier(shards, 0)
    copies = []
    for off in range(1, shards):
        peer = lax.rem(node + off, shards)
        copy = pltpu.make_async_remote_copy(
            src_ref=need_ref.at[peer], dst_ref=asked_ref.at[node],
            send_sem=send_sem.at[off - 1], recv_sem=recv_sem.at[off - 1],
            device_id=(peer, feat), device_id_type=MESH,
        )
        copy.start()
        copies.append(copy)
    own = pltpu.make_async_copy(need_ref.at[node], asked_ref.at[node], self_sem)
    own.start()
    own.wait()
    for copy in copies:
        copy.wait()


def pick_kernel(shards, asked_ref, x_ref, outbox_ref):
    for s in range(shards):

        @pl.loop(0, CAP)
        def _(k):
            columns = pl.ds(pl.multiple_of(asked_ref[s, k] * LANES, LANES), LANES)
            outbox_ref[s * CAP + k] = x_ref[:, columns]


def fetch_kernel(
    shards, feats, blocks, outbox_ref, x_ref, grad_ref, weight_ref, source_ref,
    cot_ref, full_ref, x_send, x_recv, own_sem, cot_send, cot_recv, w_send, w_recv, self_sem,
):
    node, feat = lax.axis_index("node"), lax.axis_index("feat")
    depth = x_ref.shape[0]
    per_feat = cot_ref.shape[1]
    barrier(shards, feats)
    mine = pl.ds(node * CAP, CAP)
    landing = pl.ds(blocks + node * CAP, CAP)

    copies = []
    for off in range(1, shards):
        peer = lax.rem(node + off, shards)
        copies.append(pltpu.make_async_remote_copy(
            src_ref=outbox_ref.at[pl.ds(peer * CAP, CAP)], dst_ref=source_ref.at[landing],
            send_sem=x_send.at[off - 1], recv_sem=x_recv.at[off - 1],
            device_id=(peer, feat), device_id_type=MESH,
        ))
    rows = pl.ds(pl.multiple_of(feat * depth, depth), depth)
    for off in range(1, feats):
        peer = lax.rem(feat + off, feats)
        columns = pl.ds(pl.multiple_of(peer * per_feat, per_feat), per_feat)
        for src, dst, sent, got in (
            (weight_ref, full_ref.at[rows], w_send, w_recv),
            (grad_ref.at[:, columns], cot_ref.at[rows], cot_send, cot_recv),
        ):
            copies.append(pltpu.make_async_remote_copy(
                src_ref=src, dst_ref=dst, send_sem=sent.at[off - 1], recv_sem=got.at[off - 1],
                device_id=(node, peer), device_id_type=MESH,
            ))
    own = pl.ds(pl.multiple_of(feat * per_feat, per_feat), per_feat)
    copies += [
        pltpu.make_async_copy(weight_ref, full_ref.at[rows], self_sem.at[0]),
        pltpu.make_async_copy(grad_ref.at[:, own], cot_ref.at[rows], self_sem.at[1]),
        pltpu.make_async_copy(outbox_ref.at[mine], source_ref.at[landing], self_sem.at[2]),
    ]
    for b in range(blocks):
        copies.append(pltpu.make_async_copy(
            x_ref.at[:, pl.ds(b * LANES, LANES)], source_ref.at[b], own_sem.at[b]
        ))
    for copy in copies:
        copy.start()
    for copy in copies:
        copy.wait()


def gather_kernel(steps, blocks, rows_ref, slot_ref, source_ref, mask_ref, agg_ref, deg_ref, edge_ref, acc):
    step = pl.program_id(0)
    depth = source_ref.shape[1]
    ones = jnp.ones((16, LANES), jnp.bfloat16)

    def term(g):
        t = step * GROUP + g
        edges = mask_ref[g].astype(jnp.float32).astype(jnp.bfloat16)
        edge_ref[g] = edges
        source = jnp.concatenate([source_ref[slot_ref[t]], ones], axis=0)
        return rows_ref[t], lax.dot_general(
            source, edges, (((1,), (1,)), ((), ())), preferred_element_type=jnp.float32
        )

    @pl.when(step < blocks // GROUP)
    def _():
        for g in range(GROUP):
            row, value = term(g)
            acc[row] = value

    @pl.when(step >= blocks // GROUP)
    def _():
        for g in range(0, GROUP, 2):
            row0, value0 = term(g)
            row1, value1 = term(g + 1)
            acc[row0] += value0
            acc[row1] += value1

    @pl.when(step == steps - 1)
    def _():
        for b in range(blocks):
            degree = 1.0 + acc[b, depth : depth + 1, :]
            mixed = source_ref[b].astype(jnp.float32) + acc[b, :depth, :]
            agg_ref[:, b * LANES : (b + 1) * LANES] = (mixed / degree).astype(jnp.bfloat16)
            deg_ref[b] = degree


def spread_kernel(steps, blocks, rows_ref, slot_ref, hidden_ref, deg_ref, edge_ref, own_ref, terms_ref, acc, scaled):
    step = pl.program_id(0)

    @pl.when(step == 0)
    def _():
        for b in range(blocks):
            value = hidden_ref[:, b * LANES : (b + 1) * LANES].astype(jnp.float32) / deg_ref[b]
            value = value.astype(jnp.bfloat16)
            scaled[b] = value
            acc[b] = value.astype(jnp.float32)
        acc[blocks:] = jnp.zeros_like(acc[blocks:])

    def term(g):
        t = step * GROUP + g
        return slot_ref[t], jnp.dot(
            scaled[rows_ref[t]], edge_ref[g], preferred_element_type=jnp.float32
        )

    for g in range(0, GROUP, 2):
        slot0, value0 = term(g)
        slot1, value1 = term(g + 1)
        acc[slot0] += value0
        acc[slot1] += value1

    @pl.when(step == steps - 1)
    def _():
        own_ref[...] = acc[:blocks]
        terms_ref[...] = acc[blocks:].astype(jnp.bfloat16)


def return_kernel(shards, terms_ref, back_ref, send_sem, recv_sem, self_sem):
    node, feat = lax.axis_index("node"), lax.axis_index("feat")
    barrier(shards, 0)
    copies = []
    for off in range(1, shards):
        peer = lax.rem(node + off, shards)
        copy = pltpu.make_async_remote_copy(
            src_ref=terms_ref.at[pl.ds(peer * CAP, CAP)],
            dst_ref=back_ref.at[pl.ds(node * CAP, CAP)],
            send_sem=send_sem.at[off - 1], recv_sem=recv_sem.at[off - 1],
            device_id=(peer, feat), device_id_type=MESH,
        )
        copy.start()
        copies.append(copy)
    mine = pl.ds(node * CAP, CAP)
    own = pltpu.make_async_copy(terms_ref.at[mine], back_ref.at[mine], self_sem)
    own.start()
    own.wait()
    for copy in copies:
        copy.wait()


def merge_kernel(shards, blocks, asked_ref, own_ref, back_ref, out_ref, acc):
    node = lax.axis_index("node")
    acc[...] = own_ref[...]
    for off in range(1, shards):
        peer = lax.rem(node + off, shards)

        @pl.loop(0, CAP)
        def _(k):
            acc[asked_ref[peer, k]] += back_ref[peer * CAP + k].astype(jnp.float32)

    for b in range(blocks):
        out_ref[:, b * LANES : (b + 1) * LANES] = acc[b].astype(jnp.bfloat16)


def silu_slope(value):
    sig = jax.nn.sigmoid(value)
    return sig * (1.0 + value * (1.0 - sig))


def per_device(shards, feats, x_feat, weight, out_grad, tile_rows, tile_cols, tile_masks):
    depth, local_rows = x_feat.shape
    blocks = local_rows // LANES
    tiles = tile_cols.shape[0]
    hidden = weight.shape[1]
    features = depth * feats
    per_feat = local_rows // feats
    slots = blocks + shards * CAP
    bf16, f32, i32 = jnp.bfloat16, jnp.float32, jnp.int32
    shape = jax.ShapeDtypeStruct
    dma = pltpu.SemaphoreType.DMA
    steps = tiles // GROUP

    need, slot = pl.pallas_call(
        functools.partial(plan_kernel, shards, blocks, tiles),
        out_shape=(shape((shards, LANES), i32), shape((tiles,), i32)),
        in_specs=[spec(SMEM)],
        out_specs=(spec(SMEM), spec(SMEM)),
        scratch_shapes=[SMEM((blocks * shards,), i32), SMEM((shards,), i32)],
    )(tile_cols)

    asked = pl.pallas_call(
        functools.partial(ask_kernel, shards),
        out_shape=shape((shards, 1, LANES), i32),
        in_specs=[spec(VMEM)],
        out_specs=spec(VMEM),
        scratch_shapes=[dma((shards - 1,)), dma((shards - 1,)), dma(())],
        compiler_params=params(16, collective_id=2, has_side_effects=True),
    )(need.reshape(shards, 1, LANES)).reshape(shards, LANES)

    outbox = pl.pallas_call(
        functools.partial(pick_kernel, shards),
        out_shape=shape((shards * CAP, depth, LANES), bf16),
        in_specs=[spec(SMEM), spec(VMEM)],
        out_specs=spec(VMEM),
        compiler_params=params(24),
    )(asked, x_feat)

    source, cotangent_rows, full_weight = pl.pallas_call(
        functools.partial(fetch_kernel, shards, feats, blocks),
        out_shape=(
            shape((slots, depth, LANES), bf16),
            shape((features, per_feat), bf16),
            shape((features, hidden), bf16),
        ),
        in_specs=[spec(ANY)] * 4,
        out_specs=(spec(ANY),) * 3,
        scratch_shapes=[
            dma((shards - 1,)), dma((shards - 1,)), dma((blocks,)),
            dma((feats - 1,)), dma((feats - 1,)), dma((feats - 1,)), dma((feats - 1,)),
            dma((3,)),
        ],
        compiler_params=params(24, collective_id=0, has_side_effects=True),
    )(outbox, x_feat, out_grad, weight)

    whole3 = lambda i, *_: (0, 0, 0)
    whole2 = lambda i, *_: (0, 0)
    by_tile = lambda i, *_: (i, 0, 0)
    aggregated, degree, edges = pl.pallas_call(
        functools.partial(gather_kernel, steps, blocks),
        grid_spec=pltpu.PrefetchScalarGridSpec(
            num_scalar_prefetch=2,
            grid=(steps,),
            in_specs=[
                pl.BlockSpec((slots, depth, LANES), whole3),
                pl.BlockSpec((GROUP, LANES, LANES), by_tile),
            ],
            out_specs=(
                pl.BlockSpec((depth, local_rows), whole2),
                pl.BlockSpec((blocks, 1, LANES), whole3),
                pl.BlockSpec((GROUP, LANES, LANES), by_tile),
            ),
            scratch_shapes=[VMEM((blocks, depth + 16, LANES), f32)],
        ),
        out_shape=(
            shape((depth, local_rows), bf16),
            shape((blocks, 1, LANES), f32),
            shape((tiles, LANES, LANES), bf16),
        ),
        compiler_params=params(40),
    )(tile_rows, slot, source, tile_masks)

    node_rows = lax.all_to_all(aggregated, "feat", split_axis=1, concat_axis=0, tiled=True)
    row_preact = lax.dot_general(
        full_weight, node_rows, (((0,), (0,)), ((), ())), preferred_element_type=f32
    )
    row_activ = jax.nn.silu(row_preact).astype(bf16)
    activ = lax.all_to_all(row_activ, "feat", split_axis=0, concat_axis=1, tiled=True)
    grad_rows = (cotangent_rows.astype(f32) * silu_slope(row_preact)).astype(bf16)
    row_hidden = jnp.dot(full_weight, grad_rows, preferred_element_type=f32).astype(bf16)
    hidden_grad = lax.all_to_all(row_hidden, "feat", split_axis=0, concat_axis=1, tiled=True)
    full_part = lax.dot_general(
        node_rows, grad_rows, (((1,), (1,)), ((), ())), preferred_element_type=f32
    )
    part_grad = lax.psum_scatter(full_part, "feat", scatter_dimension=0, tiled=True)
    weight_grad = lax.psum(part_grad, "node") * (local_rows * shards) ** (-0.5)

    own, terms = pl.pallas_call(
        functools.partial(spread_kernel, steps, blocks),
        grid_spec=pltpu.PrefetchScalarGridSpec(
            num_scalar_prefetch=2,
            grid=(steps,),
            in_specs=[
                pl.BlockSpec((depth, local_rows), whole2),
                pl.BlockSpec((blocks, 1, LANES), whole3),
                pl.BlockSpec((GROUP, LANES, LANES), by_tile),
            ],
            out_specs=(
                pl.BlockSpec((blocks, depth, LANES), whole3),
                pl.BlockSpec((shards * CAP, depth, LANES), whole3),
            ),
            scratch_shapes=[
                VMEM((slots, depth, LANES), f32),
                VMEM((blocks, depth, LANES), bf16),
            ],
        ),
        out_shape=(
            shape((blocks, depth, LANES), f32),
            shape((shards * CAP, depth, LANES), bf16),
        ),
        compiler_params=params(40),
    )(tile_rows, slot, hidden_grad, degree, edges)

    back = pl.pallas_call(
        functools.partial(return_kernel, shards),
        out_shape=shape((shards * CAP, depth, LANES), bf16),
        in_specs=[spec(ANY)],
        out_specs=spec(ANY),
        scratch_shapes=[dma((shards - 1,)), dma((shards - 1,)), dma(())],
        compiler_params=params(24, collective_id=1, has_side_effects=True),
    )(terms)

    x_grad = pl.pallas_call(
        functools.partial(merge_kernel, shards, blocks),
        out_shape=shape((depth, local_rows), bf16),
        in_specs=[spec(SMEM), spec(VMEM), spec(VMEM)],
        out_specs=spec(VMEM),
        scratch_shapes=[VMEM((blocks, depth, LANES), f32)],
        compiler_params=params(32),
    )(asked, own, back)
    return (activ, x_grad, weight_grad)


def solution(mesh):
    placed = (
        P("feat", "node"),
        P("feat", None),
        P("feat", "node"),
        P("node"),
        P("node"),
        P("node", None, None),
    )
    return jax.shard_map(
        functools.partial(per_device, mesh.shape["node"], mesh.shape["feat"]),
        mesh=mesh,
        in_specs=placed,
        out_specs=(P("feat", "node"), P("feat", "node"), P("feat", None)),
        check_vma=False,
    )
```

time: 351 us -> 246 us (0.70)
  waiting for transfers between devices: 187 us -> 60.4 us
  Pallas kernels: 0 us -> 119 us
  matrix products: 54.7 us -> 4.82 us
  local copies, waits for them, and re-layouts: 36.6 us -> 5.27 us
  starting transfers between devices: 12.8 us -> 3.6 us
  other arithmetic: 9.81 us -> 1.68 us
    pallas_call x0 -> x8, Pallas kernels: none -> 119 us  [the longest x1 46.7 us: per_device(): pl.pallas_call(functools.partial(return_kernel, shards), out_shape=shape(...]
    reduce_scatter x1 -> x0, waiting for transfers between devices: 89.1 us -> none  [per_device(): lax.psum_scatter(spread.astype(jnp.bfloat16), 'node', scatter_dimension=1...]
    all_gather x1 -> x0, waiting for transfers between devices: 71.3 us -> none  [per_device(): gathered = lax.all_gather(x_feat, 'node', axis=1, tiled=True)]
    dot_general x6 -> x1, matrix products: 49.3 us -> 0.71 us  [per_device(): jnp.dot(full_weight, grad_rows, preferred_element_type=f32).astype(bf16)]
    psum x1, waiting for transfers between devices: 14.4 us -> 39.3 us  [per_device(): weight_grad = lax.psum(part_grad, 'node') * (local_rows * shards) ** (-0.5)]
    reduce_scatter x1, waiting for transfers between devices: 0.01 us -> 21 us  [per_device(): lax.psum_scatter(full_part, 'feat', scatter_dimension=0, tiled=True)]
    all_to_all x1 -> x2, blocking collectives: 15.4 us -> 36.4 us  [the longest x1 18.5 us: per_device(): lax.all_to_all(aggregated, 'feat', split_axis=1, concat_axis=0, tiled=True)]
    all_gather x1 -> x0, blocking collectives: 19.9 us -> none  [per_device(): full_weight = lax.all_gather(weight, 'feat', axis=0, tiled=True)]
  transfers between devices with their start and end apart: 7 -> 3, of which waited for: 4 -> 2; matrix products, arithmetic and copies ran while one was open for 25% -> 1% of each run, Pallas kernels for 0% -> 22%
where the time goes in v1:
time: 246 us; the launch traced here: 245 us
  Pallas kernels  119 us (48%)
  waiting for transfers between devices  60.4 us (25%)
  blocking collectives  36.4 us (15%)
  between operations  14.2 us (6%)
  local copies, waits for them, and re-layouts  5.27 us (2%)
  matrix products  4.82 us (2%)
  starting transfers between devices  3.6 us (1%)
    pallas_call x1, Pallas kernels, per_device(): pl.pallas_call(functools.partial(return_kernel, shards), out_shape=shape(...  46.7 us
    psum x1, waiting for transfers between devices, per_device(): weight_grad = lax.psum(part_grad, 'node') * (local_rows * shards) ** (-0.5)  39.3 us
    pallas_call x1, Pallas kernels, per_device(): pl.pallas_call(functools.partial(fetch_kernel, shards, feats, blocks), ou...  38.2 us
    reduce_scatter x1, waiting for transfers between devices, per_device(): lax.psum_scatter(full_part, 'feat', scatter_dimension=0, tiled=True)  21 us
    all_to_all x1, blocking collectives, per_device(): lax.all_to_all(aggregated, 'feat', split_axis=1, concat_axis=0, tiled=True)  18.5 us
    all_to_all x1, blocking collectives, per_device(): lax.all_to_all(row_hidden, 'feat', split_axis=0, concat_axis=1, tiled=True)  17.9 us
    pallas_call x1, Pallas kernels, per_device(): pl.pallas_call(functools.partial(gather_kernel, steps, blocks), grid_spec...  12.1 us
    pallas_call x1, Pallas kernels, per_device(): pl.pallas_call(functools.partial(ask_kernel, shards), out_shape=shape((sh...  7.28 us
  transfers between devices with their start and end apart: 3, of which 2 were waited for; matrix products, arithmetic and copies ran while one was open for 1% of the time, Pallas kernels for 22%

profile of v1, /device:TPU:0, one launch (start us, length us, event | category | flops | bytes accessed | tf_op | source)
XLA Modules:
  0.0 245.3 jit_solution(8702580872969823257)
XLA Ops:
  7.2 0.0 reduce-scatter.2.cloned.1.call-start
  7.2 5.4 %shard_map.85 = (s32[8,128]{1,0:T(8,128)}, s32[120]{0:T(128)}) custom-call(s32[120]{0:T(128)} %cols_ref.1), custom_call_target="tpu_custom_call" | custom-call | tf_op jit(solution)/shard_map/pallas_call | solution.py:273
  12.6 0.0 copy-start.5
  12.6 0.7 copy-done.5
  13.3 7.3 %shard_map.86 = s32[8,1,128]{2,1,0:T(1,128)S(1)} custom-call(s32[8,1,128]{2,1,0:T(1,128)S(1)} %bitcast.27), custom_call_target="tpu_custom_call" | custom-call | tf_op jit(solution)/shard_map/pallas_call | solution.py:281
  20.6 0.0 copy-start
  20.6 1.2 copy-done
  21.8 0.0 copy-start.3
  21.8 0.0 copy-start.4
  21.8 1.6 shard_map.87.outbox_ref
  23.5 0.0 copy-done.3
  23.5 0.0 copy-done.4
  23.5 0.0 copy-start.6
  23.5 0.0 copy-start.7
  23.5 38.2 %shard_map.88 = (bf16[96,128,128]{2,1,0:T(8,128)(2,1)S(1)}, bf16[512,1024]{1,0:T(8,128)(2,1)S(1)}, bf16[512,512]{1,0:T(8,128)(2,1)S(1)}) custom-call(bf16[64,128,128]{2,1,0:T(8,128)(2,1)S(1)} %shard_map.87.outbox_ref, bf16[128,4096]{1,0:T(8,128)(2,1)S(1)} %copy-done, bf16[128,4096]{1,0:T(8,128)(2,1)S(1)} %copy-done.3, bf16[128,512]{1,0:T(8,128)(2,1)S(1)} %copy-done.4), custom_call_target="tpu_custom_call" | custom-call | tf_op jit(solution)/shard_map/pallas_call | solution.py:298
  61.7 0.0 copy-done.6
  61.8 0.0 copy-done.7
  61.8 12.1 %shard_map.89 = (bf16[128,4096]{1,0:T(8,128)(2,1)S(1)}, f32[32,1,128]{2,1,0:T(1,128)S(1)}, bf16[120,128,128]{2,1,0:T(8,128)(2,1)S(1)}) custom-call(s32[120]{0:T(128)S(1)} %copy-done.6, s32[120]{0:T(128)S(1)} %copy-done.7, bf16[96,128,128]{2,1,0:T(8,128)(2,1)S(1)} %get-tuple-element.16.source_ref, s32[120,128,128]{2,1,0:T(8,128)} %mask_ref.1), custom_call_target="tpu_custom_call" | custom-call | tf_op jit(solution)/shard_map/pallas_call | solution.py:318
  73.9 0.0 copy-start.1
  73.9 0.1 copy.21
  74.0 18.5 %all_to_all.57 = bf16[128,4,1024]{2,0,1:T(8,128)(2,1)S(1)} all-to-all(bf16[128,4,1024]{2,0,1:T(8,128)(2,1)S(1)} %bitcast.30), channel_id=1, replica_groups=mesh['node'=8,'feat'=4] {'feat'}, dimensions={1} | all-to-all | bytes 2097152 | tf_op jit(solution)/shard_map/all_to_all | solution.py:342
  92.5 0.0 copy-done.1
  92.5 2.4 multiply_convert_fusion
  94.9 1.7 fusion
  96.6 0.0 reduce-scatter.2.cloned.1.call-update
  96.6 0.7 convolution_convert_fusion
  97.3 17.9 %all_to_all.58 = bf16[4,128,1024]{2,1,0:T(8,128)(2,1)S(1)} all-to-all(bf16[4,128,1024]{2,1,0:T(8,128)(2,1)S(1)} %bitcast.34), channel_id=1, replica_groups=mesh['node'=8,'feat'=4] {'feat'}, dimensions={0} | all-to-all | bytes 2097152 | tf_op jit(solution)/shard_map/all_to_all | solution.py:350
  115.2 3.5 %all-to-all-start.1 = ((bf16[4,128,1024]{2,1,0:T(8,128)(2,1)}), bf16[4,128,1024]{2,1,0:T(8,128)(2,1)S(1)}, u32[]{:S(2)}, u32[]{:S(2)}) async-start(bf16[4,128,1024]{2,1,0:T(8,128)(2,1)} %bitcast.4), calls=%async_computation.1 | async-start | bytes 2097152 | tf_op jit(solution)/shard_map/all_to_all | solution.py:347
  118.7 0.0 all-reduce.2.cloned.1.call-start
  118.8 21.0 %reduce-scatter.2.cloned.1.call-done = f32[128,512]{1,0:T(8,128)} async-done(((f32[512,512]{1,0:T(8,128)}), f32[128,512]{1,0:T(8,128)}) %reduce-scatter.2.cloned.1.call-update) | async-done | bytes 262160 | tf_op jit(solution)/shard_map/reduce_scatter | solution.py:354
  139.8 0.0 all-reduce.2.cloned.1.call-update
  139.8 0.1 copy.19
  139.9 0.0 all-to-all-done.1
  139.9 1.1 copy.18
  141.0 0.0 copy-start.2
  141.0 2.1 copy-done.2
  143.1 5.0 %shard_map.90 = (f32[32,128,128]{2,1,0:T(8,128)S(1)}, bf16[64,128,128]{2,1,0:T(8,128)(2,1)S(1)}) custom-call(s32[120]{0:T(128)S(1)} %copy-done.6, s32[120]{0:T(128)S(1)} %copy-done.7, bf16[128,4096]{1,0:T(8,128)(2,1)S(1)} %bitcast.23, f32[32,1,128]{2,1,0:T(1,128)S(1)} %get-tuple-element.19.deg_ref, bf16[120,128,128]{2,1,0:T(8,128)(2,1)S(1)} %copy-done.2), custom_call_target="tpu_custom_call" | custom-call | tf_op jit(solution)/shard_map/pallas_call | solution.py:357
  148.1 46.7 %shard_map.91.back_ref = bf16[64,128,128]{2,1,0:T(8,128)(2,1)S(1)} custom-call(bf16[64,128,128]{2,1,0:T(8,128)(2,1)S(1)} %get-tuple-element.22.terms_ref), custom_call_target="tpu_custom_call" | custom-call | tf_op jit(solution)/shard_map/pallas_call | solution.py:383
  194.9 2.6 %shard_map.92 = bf16[128,4096]{1,0:T(8,128)(2,1)} custom-call(s32[8,128]{1,0:T(8,128)S(1)} %bitcast.26, f32[32,128,128]{2,1,0:T(8,128)S(1)} %get-tuple-element.21.own_ref, bf16[64,128,128]{2,1,0:T(8,128)(2,1)S(1)} %shard_map.91.back_ref), custom_call_target="tpu_custom_call" | custom-call | tf_op jit(solution)/shard_map/pallas_call | solution.py:392
  197.5 39.3 %all-reduce.2.cloned.1.call-done = f32[128,512]{1,0:T(8,128)} async-done(((f32[128,512]{1,0:T(8,128)}), f32[128,512]{1,0:T(8,128)}) %all-reduce.2.cloned.1.call-update) | async-done | bytes 262160 | tf_op jit(solution)/shard_map/psum | solution.py:355
  236.8 1.7 broadcast_multiply_fusion
Async XLA Ops:
  7.2 132.7 %reduce-scatter.2.cloned.1.call-start = ((), (), s32[]{:S(2)}) async-start(), calls=%async_computation.4 | async-start | bytes 1310720 | tf_op jit(solution)/shard_map/reduce_scatter | solution.py:354
  12.6 0.7 copy-start.5
  20.6 1.2 copy-start
  21.8 1.6 copy-start.3
  21.8 1.6 copy-start.4
  23.5 38.3 %copy-start.6 = (s32[120]{0:T(128)S(1)}, s32[120]{0:T(128)}, u32[]{:S(2)}) copy-start(s32[120]{0:T(128)} %rows_ref.3) | copy-start | bytes 1444
  23.5 38.3 %copy-start.7 = (s32[120]{0:T(128)S(1)}, s32[120]{0:T(128)}, u32[]{:S(2)}) copy-start(s32[120]{0:T(128)} %get-tuple-element.15.slot_ref) | copy-start | bytes 1444
  73.9 18.6 %copy-start.1 = (bf16[120,128,128]{2,1,0:T(8,128)(2,1)}, bf16[120,128,128]{2,1,0:T(8,128)(2,1)S(1)}, u32[]{:S(2)}) copy-start(bf16[120,128,128]{2,1,0:T(8,128)(2,1)S(1)} %get-tuple-element.20.edge_ref) | copy-start | bytes 11796484
  115.2 24.7 %all-to-all-start.1 = ((bf16[4,128,1024]{2,1,0:T(8,128)(2,1)}), bf16[4,128,1024]{2,1,0:T(8,128)(2,1)S(1)}, u32[]{:S(2)}, u32[]{:S(2)}) async-start(bf16[4,128,1024]{2,1,0:T(8,128)(2,1)} %bitcast.4), calls=%async_computation.1 | async-start | bytes 2097152 | tf_op jit(solution)/shard_map/all_to_all | solution.py:347
  118.7 118.0 %all-reduce.2.cloned.1.call-start = ((), (), s32[]{:S(2)}) async-start(), calls=%async_computation.5 | async-start | bytes 524288 | tf_op jit(solution)/shard_map/psum | solution.py:355
  141.0 2.1 copy-start.2
Sparse Core Ops, SparseCore 0:
  96.7 43.0 reduce-scatter.1
  142.2 94.4 all-reduce.1

commit v2 on v1

--- a/solution.py
+++ b/solution.py
@@ -70,7 +70,7 @@
         pl.semaphore_signal(
             sem, inc=1, device_id=(node, lax.rem(feat + off, feats)), device_id_type=MESH
         )
-    pl.semaphore_wait(sem, shards - 1 + (feats - 1 if feats else 0))
+    pl.semaphore_wait(sem, max(shards - 1, 0) + max(feats - 1, 0))
 
 
 def ask_kernel(shards, need_ref, asked_ref, send_sem, recv_sem, self_sem):
@@ -216,24 +216,117 @@
         terms_ref[...] = acc[blocks:].astype(jnp.bfloat16)
 
 
-def return_kernel(shards, terms_ref, back_ref, send_sem, recv_sem, self_sem):
+def band(index, size):
+    return pl.ds(pl.multiple_of(index * size, size), size)
+
+
+def swap_kernel(feats, to_columns, src_ref, dst_ref, send_sem, recv_sem, self_sem):
     node, feat = lax.axis_index("node"), lax.axis_index("feat")
-    barrier(shards, 0)
+    barrier(0, feats)
+    depth = min(src_ref.shape[0], dst_ref.shape[0])
+    width = min(src_ref.shape[1], dst_ref.shape[1])
+
+    def ends(peer):
+        if to_columns:
+            return src_ref.at[band(peer, depth)], dst_ref.at[:, band(feat, width)]
+        return src_ref.at[:, band(peer, width)], dst_ref.at[band(feat, depth)]
+
     copies = []
+    for off in range(1, feats):
+        peer = lax.rem(feat + off, feats)
+        src, dst = ends(peer)
+        copies.append(pltpu.make_async_remote_copy(
+            src_ref=src, dst_ref=dst, send_sem=send_sem.at[off - 1],
+            recv_sem=recv_sem.at[off - 1], device_id=(node, peer), device_id_type=MESH,
+        ))
+    src, dst = ends(feat)
+    copies.append(pltpu.make_async_copy(src, dst, self_sem))
+    for copy in copies:
+        copy.start()
+    for copy in copies:
+        copy.wait()
+
+
+def return_kernel(
+    shards, feats, scale, terms_ref, rows_ref, part_ref, back_ref, activ_ref, grad_ref,
+    feat_in, partial, node_in, reduced, gathered, z_send, z_recv, a_send, a_recv, self_sem,
+    p_send, p_recv, q_send, q_recv, r_send, r_recv,
+):
+    node, feat = lax.axis_index("node"), lax.axis_index("feat")
+    depth = activ_ref.shape[0]
+    width = rows_ref.shape[1]
+    barrier(shards, feats)
+
+    parts = []
+    for off in range(1, feats):
+        peer = lax.rem(feat + off, feats)
+        parts.append(pltpu.make_async_remote_copy(
+            src_ref=part_ref.at[peer], dst_ref=feat_in.at[off - 1],
+            send_sem=p_send.at[off - 1], recv_sem=p_recv.at[off - 1],
+            device_id=(node, peer), device_id_type=MESH,
+        ))
+    copies = []
     for off in range(1, shards):
         peer = lax.rem(node + off, shards)
-        copy = pltpu.make_async_remote_copy(
+        copies.append(pltpu.make_async_remote_copy(
             src_ref=terms_ref.at[pl.ds(peer * CAP, CAP)],
             dst_ref=back_ref.at[pl.ds(node * CAP, CAP)],
-            send_sem=send_sem.at[off - 1], recv_sem=recv_sem.at[off - 1],
+            send_sem=z_send.at[off - 1], recv_sem=z_recv.at[off - 1],
             device_id=(peer, feat), device_id_type=MESH,
-        )
+        ))
+    for off in range(1, feats):
+        peer = lax.rem(feat + off, feats)
+        copies.append(pltpu.make_async_remote_copy(
+            src_ref=rows_ref.at[band(peer, depth)], dst_ref=activ_ref.at[:, band(feat, width)],
+            send_sem=a_send.at[off - 1], recv_sem=a_recv.at[off - 1],
+            device_id=(node, peer), device_id_type=MESH,
+        ))
+    mine = pl.ds(node * CAP, CAP)
+    copies += [
+        pltpu.make_async_copy(terms_ref.at[mine], back_ref.at[mine], self_sem.at[0]),
+        pltpu.make_async_copy(
+            rows_ref.at[band(feat, depth)], activ_ref.at[:, band(feat, width)], self_sem.at[1]
+        ),
+    ]
+    for copy in parts + copies:
         copy.start()
-        copies.append(copy)
-    mine = pl.ds(node * CAP, CAP)
-    own = pltpu.make_async_copy(terms_ref.at[mine], back_ref.at[mine], self_sem)
-    own.start()
-    own.wait()
+
+    for copy in parts:
+        copy.wait()
+    total = part_ref[feat].astype(jnp.float32)
+    for i in range(feats - 1):
+        total += feat_in[i].astype(jnp.float32)
+    partial[...] = total.astype(jnp.bfloat16)
+    slices = []
+    for off in range(1, shards):
+        peer = lax.rem(node + off, shards)
+        slices.append(pltpu.make_async_remote_copy(
+            src_ref=partial.at[peer], dst_ref=node_in.at[off - 1],
+            send_sem=q_send.at[off - 1], recv_sem=q_recv.at[off - 1],
+            device_id=(peer, feat), device_id_type=MESH,
+        ))
+    for copy in slices:
+        copy.start()
+    for copy in slices:
+        copy.wait()
+    total = partial[node].astype(jnp.float32)
+    for i in range(shards - 1):
+        total += node_in[i].astype(jnp.float32)
+    reduced[...] = total.astype(jnp.bfloat16)
+    spreads = []
+    for off in range(1, shards):
+        peer = lax.rem(node + off, shards)
+        spreads.append(pltpu.make_async_remote_copy(
+            src_ref=reduced, dst_ref=gathered.at[node],
+            send_sem=r_send.at[off - 1], recv_sem=r_recv.at[off - 1],
+            device_id=(peer, feat), device_id_type=MESH,
+        ))
+    for copy in spreads:
+        copy.start()
+    gathered[node] = reduced[...]
+    for copy in spreads:
+        copy.wait()
+    grad_ref[...] = gathered[...].astype(jnp.float32) * scale
     for copy in copies:
         copy.wait()
 
@@ -339,20 +432,30 @@
         compiler_params=params(40),
     )(tile_rows, slot, source, tile_masks)
 
-    node_rows = lax.all_to_all(aggregated, "feat", split_axis=1, concat_axis=0, tiled=True)
+    def swap(array, to_columns, number):
+        wide = (depth, local_rows) if to_columns else (features, per_feat)
+        return pl.pallas_call(
+            functools.partial(swap_kernel, feats, to_columns),
+            out_shape=shape(wide, bf16),
+            in_specs=[spec(ANY)],
+            out_specs=spec(ANY),
+            scratch_shapes=[dma((feats - 1,)), dma((feats - 1,)), dma(())],
+            compiler_params=params(24, collective_id=number, has_side_effects=True),
+        )(array)
+
+    node_rows = swap(aggregated, False, 3)
     row_preact = lax.dot_general(
         full_weight, node_rows, (((0,), (0,)), ((), ())), preferred_element_type=f32
     )
     row_activ = jax.nn.silu(row_preact).astype(bf16)
-    activ = lax.all_to_all(row_activ, "feat", split_axis=0, concat_axis=1, tiled=True)
     grad_rows = (cotangent_rows.astype(f32) * silu_slope(row_preact)).astype(bf16)
     row_hidden = jnp.dot(full_weight, grad_rows, preferred_element_type=f32).astype(bf16)
-    hidden_grad = lax.all_to_all(row_hidden, "feat", split_axis=0, concat_axis=1, tiled=True)
     full_part = lax.dot_general(
         node_rows, grad_rows, (((1,), (1,)), ((), ())), preferred_element_type=f32
     )
-    part_grad = lax.psum_scatter(full_part, "feat", scatter_dimension=0, tiled=True)
-    weight_grad = lax.psum(part_grad, "node") * (local_rows * shards) ** (-0.5)
+    slice_rows = depth // shards
+    full_part = full_part.astype(bf16).reshape(feats, shards, slice_rows, hidden)
+    hidden_grad = swap(row_hidden, True, 4)
 
     own, terms = pl.pallas_call(
         functools.partial(spread_kernel, steps, blocks),
@@ -380,14 +483,26 @@
         compiler_params=params(40),
     )(tile_rows, slot, hidden_grad, degree, edges)
 
-    back = pl.pallas_call(
-        functools.partial(return_kernel, shards),
-        out_shape=shape((shards * CAP, depth, LANES), bf16),
-        in_specs=[spec(ANY)],
-        out_specs=spec(ANY),
-        scratch_shapes=[dma((shards - 1,)), dma((shards - 1,)), dma(())],
+    piece = (slice_rows, hidden)
+    back, activ, weight_grad = pl.pallas_call(
+        functools.partial(return_kernel, shards, feats, (local_rows * shards) ** (-0.5)),
+        out_shape=(
+            shape((shards * CAP, depth, LANES), bf16),
+            shape((depth, local_rows), bf16),
+            shape((shards, *piece), f32),
+        ),
+        in_specs=[spec(ANY), spec(ANY), spec(VMEM)],
+        out_specs=(spec(ANY), spec(ANY), spec(VMEM)),
+        scratch_shapes=[
+            VMEM((feats - 1, shards, *piece), bf16), VMEM((shards, *piece), bf16),
+            VMEM((shards - 1, *piece), bf16), VMEM(piece, bf16), VMEM((shards, *piece), bf16),
+            dma((shards - 1,)), dma((shards - 1,)), dma((feats - 1,)), dma((feats - 1,)), dma((2,)),
+            dma((feats - 1,)), dma((feats - 1,)), dma((shards - 1,)), dma((shards - 1,)),
+            dma((shards - 1,)), dma((shards - 1,)),
+        ],
         compiler_params=params(24, collective_id=1, has_side_effects=True),
-    )(terms)
+    )(terms, row_activ, full_part)
+    weight_grad = weight_grad.reshape(depth, hidden)
 
     x_grad = pl.pallas_call(
         functools.partial(merge_kernel, shards, blocks),

time: 246 us -> 177 us (0.72)
  waiting for transfers between devices: 60.4 us -> 0 us
  Pallas kernels: 119 us -> 170 us
  blocking collectives: 36.4 us -> 0 us
  between operations: 14.2 us -> 0.79 us
  starting transfers between devices: 3.6 us -> 0 us
    pallas_call x1 -> x3, Pallas kernels: 46.7 us -> 97.1 us  [the longest x1 66.4 us: per_device(): pl.pallas_call(functools.partial(return_kernel, shards, feats, (local_row...]
    psum x1 -> x0, waiting for transfers between devices: 39.3 us -> none  [per_device(): weight_grad = lax.psum(part_grad, 'node') * (local_rows * shards) ** (-0.5)]
    all_to_all x2 -> x0, blocking collectives: 36.4 us -> none  [the longest x1 18.5 us: per_device(): lax.all_to_all(aggregated, 'feat', split_axis=1, concat_axis=0, tiled=True)]
    reduce_scatter x1 -> x0, waiting for transfers between devices: 21 us -> none  [per_device(): lax.psum_scatter(full_part, 'feat', scatter_dimension=0, tiled=True)]
    all_to_all x1 -> x0, starting transfers between devices: 3.52 us -> none  [per_device(): lax.all_to_all(row_activ, 'feat', split_axis=0, concat_axis=1, tiled=True)]
  transfers between devices with their start and end apart: 3 -> 0, of which waited for: 2 -> 0; matrix products, arithmetic and copies ran while one was open for 1% -> 0% of each run, Pallas kernels for 22% -> 0%
where the time goes in v2:
time: 177 us
  Pallas kernels  170 us (96%)
  local copies, waits for them, and re-layouts  3.59 us (2%)
  matrix products  2.9 us (2%)
    pallas_call x1, Pallas kernels, per_device(): pl.pallas_call(functools.partial(return_kernel, shards, feats, (local_row...  66.4 us
    pallas_call x1, Pallas kernels, per_device(): pl.pallas_call(functools.partial(fetch_kernel, shards, feats, blocks), ou...  38.2 us
    pallas_call x2, Pallas kernels, swap(): pl.pallas_call(functools.partial(swap_kernel, feats, to_columns), out_sha...  30.8 us
    pallas_call x1, Pallas kernels, per_device(): pl.pallas_call(functools.partial(gather_kernel, steps, blocks), grid_spec...  12.1 us
    pallas_call x1, Pallas kernels, per_device(): pl.pallas_call(functools.partial(ask_kernel, shards), out_shape=shape((sh...  7.28 us
    pallas_call x1, Pallas kernels, per_device(): pl.pallas_call(functools.partial(plan_kernel, shards, blocks, tiles), out...  5.39 us
    pallas_call x1, Pallas kernels, per_device(): pl.pallas_call(functools.partial(spread_kernel, steps, blocks), grid_spec...  5.21 us
    unnamed x14, local copies, waits for them, and re-layouts  3.59 us

profile of v2, /device:TPU:0, one launch (start us, length us, event | category | flops | bytes accessed | tf_op | source)
XLA Modules:
  0.0 176.9 jit_solution(16231405830346674348)
XLA Ops:
  0.6 5.4 %shard_map.85 = (s32[8,128]{1,0:T(8,128)}, s32[120]{0:T(128)}) custom-call(s32[120]{0:T(128)} %cols_ref.1), custom_call_target="tpu_custom_call" | custom-call | tf_op jit(solution)/shard_map/pallas_call | solution.py:366
  6.0 0.0 copy-start.3
  6.0 0.7 copy-done.3
  6.7 7.3 %shard_map.86 = s32[8,1,128]{2,1,0:T(1,128)S(1)} custom-call(s32[8,1,128]{2,1,0:T(1,128)S(1)} %bitcast.14), custom_call_target="tpu_custom_call" | custom-call | tf_op jit(solution)/shard_map/pallas_call | solution.py:374
  14.0 0.0 copy-start
  14.0 1.2 copy-done
  15.2 0.0 copy-start.1
  15.2 0.0 copy-start.2
  15.2 1.6 shard_map.87.outbox_ref
  16.9 0.0 copy-done.1
  16.9 0.0 copy-done.2
  16.9 0.0 copy-start.4
  16.9 0.0 copy-start.5
  16.9 38.2 %shard_map.88 = (bf16[96,128,128]{2,1,0:T(8,128)(2,1)S(1)}, bf16[512,1024]{1,0:T(8,128)(2,1)S(1)}, bf16[512,512]{1,0:T(8,128)(2,1)S(1)}) custom-call(bf16[64,128,128]{2,1,0:T(8,128)(2,1)S(1)} %shard_map.87.outbox_ref, bf16[128,4096]{1,0:T(8,128)(2,1)S(1)} %copy-done, bf16[128,4096]{1,0:T(8,128)(2,1)S(1)} %copy-done.1, bf16[128,512]{1,0:T(8,128)(2,1)S(1)} %copy-done.2), custom_call_target="tpu_custom_call" | custom-call | tf_op jit(solution)/shard_map/pallas_call | solution.py:391
  55.2 0.0 copy-done.4
  55.2 0.0 copy-done.5
  55.2 12.1 %shard_map.89 = (bf16[128,4096]{1,0:T(8,128)(2,1)S(1)}, f32[32,1,128]{2,1,0:T(1,128)S(1)}, bf16[120,128,128]{2,1,0:T(8,128)(2,1)S(1)}) custom-call(s32[120]{0:T(128)S(1)} %copy-done.4, s32[120]{0:T(128)S(1)} %copy-done.5, bf16[96,128,128]{2,1,0:T(8,128)(2,1)S(1)} %get-tuple-element.20.source_ref, s32[120,128,128]{2,1,0:T(8,128)} %mask_ref.1), custom_call_target="tpu_custom_call" | custom-call | tf_op jit(solution)/shard_map/pallas_call | solution.py:411
  67.3 15.8 %shard_map.90 = bf16[512,1024]{1,0:T(8,128)(2,1)S(1)} custom-call(bf16[128,4096]{1,0:T(8,128)(2,1)S(1)} %get-tuple-element.21.src_ref), custom_call_target="tpu_custom_call" | custom-call | tf_op jit(solution)/shard_map/pallas_call | solution.py:437
  83.1 1.4 multiply_convert_fusion
  84.6 0.7 convolution_convert_fusion.1
  85.3 0.7 convolution_convert_fusion.src_ref
  86.0 15.0 %shard_map.91.hidden_ref = bf16[128,4096]{1,0:T(8,128)(2,1)S(1)} custom-call(bf16[512,1024]{1,0:T(8,128)(2,1)S(1)} %convolution_convert_fusion.src_ref), custom_call_target="tpu_custom_call" | custom-call | tf_op jit(solution)/shard_map/pallas_call | solution.py:437
  101.0 5.2 %shard_map.92 = (f32[32,128,128]{2,1,0:T(8,128)S(1)}, bf16[64,128,128]{2,1,0:T(8,128)(2,1)S(1)}) custom-call(s32[120]{0:T(128)S(1)} %copy-done.4, s32[120]{0:T(128)S(1)} %copy-done.5, bf16[128,4096]{1,0:T(8,128)(2,1)S(1)} %shard_map.91.hidden_ref, f32[32,1,128]{2,1,0:T(1,128)S(1)} %get-tuple-element.22.deg_ref, ...), custom_call_target="tpu_custom_call" | custom-call | tf_op jit(solution)/shard_map/pallas_call | solution.py:460
  106.2 66.4 %shard_map.93 = (bf16[64,128,128]{2,1,0:T(8,128)(2,1)S(1)}, bf16[128,4096]{1,0:T(8,128)(2,1)S(1)}, f32[8,16,512]{2,1,0:T(8,128)S(1)}) custom-call(bf16[64,128,128]{2,1,0:T(8,128)(2,1)S(1)} %get-tuple-element.24.terms_ref, bf16[512,1024]{1,0:T(8,128)(2,1)S(1)} %get-tuple-element.29.rows_ref, bf16[4,8,16,512]{3,2,1,0:T(8,128)(2,1)S(1)} %bitcast.10), custom_call_target="tpu_custom_call" | custom-call | tf_op jit(solution)/shard_map/pallas_call | solution.py:487
  172.6 2.6 %shard_map.94 = bf16[128,4096]{1,0:T(8,128)(2,1)} custom-call(s32[8,128]{1,0:T(8,128)S(1)} %bitcast.13, f32[32,128,128]{2,1,0:T(8,128)S(1)} %get-tuple-element.26.own_ref, bf16[64,128,128]{2,1,0:T(8,128)(2,1)S(1)} %get-tuple-element.27.back_ref), custom_call_target="tpu_custom_call" | custom-call | tf_op jit(solution)/shard_map/pallas_call | solution.py:507
  175.2 1.0 copy.11
  176.2 0.7 copy.12
Async XLA Ops:
  6.0 0.7 copy-start.3
  14.0 1.2 copy-start
  15.2 1.6 copy-start.1
  15.2 1.6 copy-start.2
  16.9 38.3 %copy-start.4 = (s32[120]{0:T(128)S(1)}, s32[120]{0:T(128)}, u32[]{:S(2)}) copy-start(s32[120]{0:T(128)} %rows_ref.3) | copy-start | bytes 1444
  16.9 38.3 %copy-start.5 = (s32[120]{0:T(128)S(1)}, s32[120]{0:T(128)}, u32[]{:S(2)}) copy-start(s32[120]{0:T(128)} %get-tuple-element.16.slot_ref) | copy-start | bytes 1444

commit v3 on v2

--- a/solution.py
+++ b/solution.py
@@ -22,41 +22,6 @@
 
 def params(limit_mib, **more):
     return pltpu.CompilerParams(vmem_limit_bytes=limit_mib << 20, **more)
-
-
-def plan_kernel(shards, blocks, tiles, cols_ref, need_ref, slot_ref, pos, count):
-    me = lax.axis_index("node")
-
-    @pl.loop(0, shards)
-    def _(s):
-        count[s] = 0
-        for k in range(CAP):
-            need_ref[s, k] = 0
-
-    @pl.loop(0, tiles)
-    def _(t):
-        pos[cols_ref[t]] = -1
-
-    @pl.loop(0, tiles)
-    def _(t):
-        col = cols_ref[t]
-        shard = col // blocks
-        local = col - shard * blocks
-
-        @pl.when(shard == me)
-        def _():
-            slot_ref[t] = local
-
-        @pl.when(shard != me)
-        def _():
-            @pl.when(pos[col] < 0)
-            def _():
-                fresh = count[shard]
-                pos[col] = fresh
-                count[shard] = fresh + 1
-                need_ref[shard, fresh] = local
-
-            slot_ref[t] = blocks + shard * CAP + pos[col]
 
 
 def barrier(shards, feats):
@@ -73,21 +38,49 @@
     pl.semaphore_wait(sem, max(shards - 1, 0) + max(feats - 1, 0))
 
 
-def ask_kernel(shards, need_ref, asked_ref, send_sem, recv_sem, self_sem):
+def ask_kernel(
+    shards, blocks, cols_ref, asked_ref, slot_ref, need, send_sem, recv_sem, self_sem
+):
     node, feat = lax.axis_index("node"), lax.axis_index("feat")
     barrier(shards, 0)
+    columns, tiles = shards * blocks, cols_ref.shape[1]
+    f32, bf16 = jnp.float32, jnp.bfloat16
+
+    def iota(dims, axis):
+        return lax.broadcasted_iota(jnp.int32, dims, axis)
+
+    def contract_columns(left, right):
+        return lax.dot_general(left, right, (((0,), (0,)), ((), ())), preferred_element_type=f32)
+
+    hits = (iota((columns, tiles), 0) == cols_ref[...]).astype(f32)
+    present = jnp.minimum(jnp.sum(hits, axis=1, keepdims=True), 1.0)
+    present = jnp.broadcast_to(present, (columns, LANES))
+    below, above = iota((columns, columns), 0), iota((columns, columns), 1)
+    earlier = ((below < above) & (below // blocks == above // blocks)).astype(f32).astype(bf16)
+    order = contract_columns(earlier, present.astype(bf16))
+    column, lane = iota((columns, LANES), 0), iota((columns, LANES), 1)
+    shard = column // blocks
+    local = (column - shard * blocks).astype(f32)
+    chosen = jnp.where(order == lane.astype(f32), present * local, 0.0).astype(bf16)
+    of_shard = (iota((columns, LANES), 0) // blocks == iota((columns, LANES), 1)).astype(f32)
+    lists = contract_columns(of_shard.astype(bf16), chosen).astype(jnp.int32)
+    for s in range(shards):
+        need[s] = lists[s : s + 1]
     copies = []
     for off in range(1, shards):
         peer = lax.rem(node + off, shards)
         copy = pltpu.make_async_remote_copy(
-            src_ref=need_ref.at[peer], dst_ref=asked_ref.at[node],
+            src_ref=need.at[peer], dst_ref=asked_ref.at[node],
             send_sem=send_sem.at[off - 1], recv_sem=recv_sem.at[off - 1],
             device_id=(peer, feat), device_id_type=MESH,
         )
         copy.start()
         copies.append(copy)
-    own = pltpu.make_async_copy(need_ref.at[node], asked_ref.at[node], self_sem)
+    own = pltpu.make_async_copy(need.at[node], asked_ref.at[node], self_sem)
     own.start()
+    away = order + (shard * CAP + blocks).astype(f32)
+    place = jnp.where(shard == node, local, jnp.minimum(away, 255.0)).astype(bf16)
+    slot_ref[...] = contract_columns(place, hits.astype(bf16))[:1].astype(jnp.int32)
     own.wait()
     for copy in copies:
         copy.wait()
@@ -103,8 +96,8 @@
 
 
 def fetch_kernel(
-    shards, feats, blocks, outbox_ref, x_ref, grad_ref, weight_ref, source_ref,
-    cot_ref, full_ref, x_send, x_recv, own_sem, cot_send, cot_recv, w_send, w_recv, self_sem,
+    shards, feats, blocks, outbox_ref, x_ref, grad_ref, weight_ref, mask_ref, source_ref,
+    cot_ref, full_ref, edge_ref, turned_ref, masks, edges, turned, mask_sem, x_send, x_recv, own_sem, cot_send, cot_recv, w_send, w_recv, self_sem,
 ):
     node, feat = lax.axis_index("node"), lax.axis_index("feat")
     depth = x_ref.shape[0]
@@ -143,25 +136,38 @@
         copies.append(pltpu.make_async_copy(
             x_ref.at[:, pl.ds(b * LANES, LANES)], source_ref.at[b], own_sem.at[b]
         ))
+    load = pltpu.make_async_copy(mask_ref, masks, mask_sem.at[0])
+    load.start()
     for copy in copies:
         copy.start()
-    for copy in copies:
-        copy.wait()
-
-
-def gather_kernel(steps, blocks, rows_ref, slot_ref, source_ref, mask_ref, agg_ref, deg_ref, edge_ref, acc):
+    load.wait()
+
+    @pl.loop(0, masks.shape[0] // GROUP)
+    def _(i):
+        for g in range(GROUP):
+            value = masks[i * GROUP + g].astype(jnp.float32)
+            edges[i * GROUP + g] = value.astype(jnp.bfloat16)
+            turned[i * GROUP + g] = value.T.astype(jnp.bfloat16)
+
+    stores = [
+        pltpu.make_async_copy(edges, edge_ref, mask_sem.at[1]),
+        pltpu.make_async_copy(turned, turned_ref, mask_sem.at[2]),
+    ]
+    for copy in stores:
+        copy.start()
+    for copy in stores + copies:
+        copy.wait()
+
+
+def gather_kernel(steps, blocks, rows_ref, slot_ref, source_ref, turned_ref, agg_ref, deg_ref, acc):
     step = pl.program_id(0)
     depth = source_ref.shape[1]
     ones = jnp.ones((16, LANES), jnp.bfloat16)
 
     def term(g):
         t = step * GROUP + g
-        edges = mask_ref[g].astype(jnp.float32).astype(jnp.bfloat16)
-        edge_ref[g] = edges
         source = jnp.concatenate([source_ref[slot_ref[t]], ones], axis=0)
-        return rows_ref[t], lax.dot_general(
-            source, edges, (((1,), (1,)), ((), ())), preferred_element_type=jnp.float32
-        )
+        return rows_ref[t], jnp.dot(source, turned_ref[g], preferred_element_type=jnp.float32)
 
     @pl.when(step < blocks // GROUP)
     def _():
@@ -363,22 +369,17 @@
     dma = pltpu.SemaphoreType.DMA
     steps = tiles // GROUP
 
-    need, slot = pl.pallas_call(
-        functools.partial(plan_kernel, shards, blocks, tiles),
-        out_shape=(shape((shards, LANES), i32), shape((tiles,), i32)),
-        in_specs=[spec(SMEM)],
-        out_specs=(spec(SMEM), spec(SMEM)),
-        scratch_shapes=[SMEM((blocks * shards,), i32), SMEM((shards,), i32)],
-    )(tile_cols)
-
-    asked = pl.pallas_call(
-        functools.partial(ask_kernel, shards),
-        out_shape=shape((shards, 1, LANES), i32),
+    asked, slot = pl.pallas_call(
+        functools.partial(ask_kernel, shards, blocks),
+        out_shape=(shape((shards, 1, LANES), i32), shape((1, tiles), i32)),
         in_specs=[spec(VMEM)],
-        out_specs=spec(VMEM),
-        scratch_shapes=[dma((shards - 1,)), dma((shards - 1,)), dma(())],
+        out_specs=(spec(VMEM), spec(VMEM)),
+        scratch_shapes=[
+            VMEM((shards, 1, LANES), i32), dma((shards - 1,)), dma((shards - 1,)), dma(()),
+        ],
         compiler_params=params(16, collective_id=2, has_side_effects=True),
-    )(need.reshape(shards, 1, LANES)).reshape(shards, LANES)
+    )(tile_cols.reshape(1, tiles))
+    asked, slot = asked.reshape(shards, LANES), slot.reshape(tiles)
 
     outbox = pl.pallas_call(
         functools.partial(pick_kernel, shards),
@@ -388,27 +389,31 @@
         compiler_params=params(24),
     )(asked, x_feat)
 
-    source, cotangent_rows, full_weight = pl.pallas_call(
+    source, cotangent_rows, full_weight, edges, turned = pl.pallas_call(
         functools.partial(fetch_kernel, shards, feats, blocks),
         out_shape=(
             shape((slots, depth, LANES), bf16),
             shape((features, per_feat), bf16),
             shape((features, hidden), bf16),
-        ),
-        in_specs=[spec(ANY)] * 4,
-        out_specs=(spec(ANY),) * 3,
+            shape((tiles, LANES, LANES), bf16),
+            shape((tiles, LANES, LANES), bf16),
+        ),
+        in_specs=[spec(ANY)] * 5,
+        out_specs=(spec(ANY),) * 5,
         scratch_shapes=[
+            VMEM((tiles, LANES, LANES), i32),
+            VMEM((tiles, LANES, LANES), bf16), VMEM((tiles, LANES, LANES), bf16), dma((3,)),
             dma((shards - 1,)), dma((shards - 1,)), dma((blocks,)),
             dma((feats - 1,)), dma((feats - 1,)), dma((feats - 1,)), dma((feats - 1,)),
             dma((3,)),
         ],
-        compiler_params=params(24, collective_id=0, has_side_effects=True),
-    )(outbox, x_feat, out_grad, weight)
+        compiler_params=params(40, collective_id=0, has_side_effects=True),
+    )(outbox, x_feat, out_grad, weight, tile_masks)
 
     whole3 = lambda i, *_: (0, 0, 0)
     whole2 = lambda i, *_: (0, 0)
     by_tile = lambda i, *_: (i, 0, 0)
-    aggregated, degree, edges = pl.pallas_call(
+    aggregated, degree = pl.pallas_call(
         functools.partial(gather_kernel, steps, blocks),
         grid_spec=pltpu.PrefetchScalarGridSpec(
             num_scalar_prefetch=2,
@@ -420,17 +425,15 @@
             out_specs=(
                 pl.BlockSpec((depth, local_rows), whole2),
                 pl.BlockSpec((blocks, 1, LANES), whole3),
-                pl.BlockSpec((GROUP, LANES, LANES), by_tile),
             ),
             scratch_shapes=[VMEM((blocks, depth + 16, LANES), f32)],
         ),
         out_shape=(
             shape((depth, local_rows), bf16),
             shape((blocks, 1, LANES), f32),
-            shape((tiles, LANES, LANES), bf16),
         ),
         compiler_params=params(40),
-    )(tile_rows, slot, source, tile_masks)
+    )(tile_rows, slot, source, turned)
 
     def swap(array, to_columns, number):
         wide = (depth, local_rows) if to_columns else (features, per_feat)

time: 177 us -> 168 us (0.949)
  Pallas kernels: 170 us -> 158 us
  local copies, waits for them, and re-layouts: 3.59 us -> 5.66 us
    pallas_call x1, Pallas kernels: 12.1 us -> 5.8 us  [per_device(): pl.pallas_call(functools.partial(gather_kernel, steps, blocks), grid_spec...]
    pallas_call x2 -> x1, Pallas kernels: 12.7 us -> 7.71 us  [per_device(): pl.pallas_call(functools.partial(ask_kernel, shards, blocks), out_shape=(...]
    unnamed x14 -> x16, local copies, waits for them, and re-layouts: 3.59 us -> 5.66 us
where the time goes in v3:
time: 168 us
  Pallas kernels  158 us (94%)
  local copies, waits for them, and re-layouts  5.66 us (3%)
  matrix products  2.92 us (2%)
    pallas_call x1, Pallas kernels, per_device(): pl.pallas_call(functools.partial(return_kernel, shards, feats, (local_row...  66.3 us
    pallas_call x1, Pallas kernels, per_device(): pl.pallas_call(functools.partial(fetch_kernel, shards, feats, blocks), ou...  38.3 us
    pallas_call x2, Pallas kernels, swap(): pl.pallas_call(functools.partial(swap_kernel, feats, to_columns), out_sha...  30.9 us
    pallas_call x1, Pallas kernels, per_device(): pl.pallas_call(functools.partial(ask_kernel, shards, blocks), out_shape=(...  7.71 us
    pallas_call x1, Pallas kernels, per_device(): pl.pallas_call(functools.partial(gather_kernel, steps, blocks), grid_spec...  5.8 us
    unnamed x16, local copies, waits for them, and re-layouts  5.66 us
    pallas_call x1, Pallas kernels, per_device(): pl.pallas_call(functools.partial(spread_kernel, steps, blocks), grid_spec...  5.21 us

profile of v3, /device:TPU:0, one launch (start us, length us, event | category | flops | bytes accessed | tf_op | source)
XLA Modules:
  0.0 167.8 jit_solution(16196672966794459261)
XLA Ops:
  0.6 0.0 copy-start.6
  0.6 0.6 copy-done.6
  1.3 7.7 %shard_map.85 = (s32[8,1,128]{2,1,0:T(1,128)S(1)}, s32[1,120]{1,0:T(1,128)S(1)}) custom-call(s32[1,120]{1,0:T(1,128)S(1)} %bitcast.17), custom_call_target="tpu_custom_call" | custom-call | tf_op jit(solution)/shard_map/pallas_call | solution.py:372
  9.0 0.0 copy-start
  9.0 1.2 copy-done
  10.2 0.0 copy-start.1
  10.2 0.0 copy-start.3
  10.2 0.0 copy-start.4
  10.2 1.6 shard_map.86.outbox_ref
  11.9 0.0 copy-done.1
  11.9 0.0 copy-done.3
  11.9 0.0 copy-done.4
  11.9 0.0 copy-start.5
  11.9 38.3 %shard_map.87 = (bf16[96,128,128]{2,1,0:T(8,128)(2,1)S(1)}, bf16[512,1024]{1,0:T(8,128)(2,1)S(1)}, bf16[512,512]{1,0:T(8,128)(2,1)S(1)}, bf16[120,128,128]{2,1,0:T(8,128)(2,1)S(1)}, bf16[120,128,128]{2,1,0:T(8,128)(2,1)}) custom-call(bf16[64,128,128]{2,1,0:T(8,128)(2,1)S(1)} %shard_map.86.outbox_ref, bf16[128,4096]{1,0:T(8,128)(2,1)S(1)} %copy-done.1, ...), custom_call_target="tpu_custom_call" | custom-call | tf_op jit(solution)/shard_map/pallas_call | solution.py:392
  50.2 0.0 copy-done.5
  50.2 0.0 copy-start.2
  50.2 2.1 %copy-done.2 = bf16[120,128,128]{2,1,0:T(8,128)(2,1)S(1)} copy-done((bf16[120,128,128]{2,1,0:T(8,128)(2,1)S(1)}, bf16[120,128,128]{2,1,0:T(8,128)(2,1)}, u32[]{:S(2)}) %copy-start.2) | copy-done | bytes 3932184
  52.3 5.8 %shard_map.88 = (bf16[128,4096]{1,0:T(8,128)(2,1)S(1)}, f32[32,1,128]{2,1,0:T(1,128)S(1)}) custom-call(s32[120]{0:T(128)S(1)} %copy-done.5, s32[120]{0:T(128)S(1)} %bitcast.15, bf16[96,128,128]{2,1,0:T(8,128)(2,1)S(1)} %get-tuple-element.21.source_ref, bf16[120,128,128]{2,1,0:T(8,128)(2,1)S(1)} %copy-done.2), custom_call_target="tpu_custom_call" | custom-call | tf_op jit(solution)/shard_map/pallas_call | solution.py:416
  58.1 15.8 %shard_map.89 = bf16[512,1024]{1,0:T(8,128)(2,1)S(1)} custom-call(bf16[128,4096]{1,0:T(8,128)(2,1)S(1)} %get-tuple-element.23.src_ref), custom_call_target="tpu_custom_call" | custom-call | tf_op jit(solution)/shard_map/pallas_call | solution.py:440
  73.9 1.4 multiply_convert_fusion
  75.4 0.7 convolution_convert_fusion.1
  76.1 0.7 convolution_convert_fusion.src_ref
  76.9 15.1 %shard_map.90.hidden_ref = bf16[128,4096]{1,0:T(8,128)(2,1)S(1)} custom-call(bf16[512,1024]{1,0:T(8,128)(2,1)S(1)} %convolution_convert_fusion.src_ref), custom_call_target="tpu_custom_call" | custom-call | tf_op jit(solution)/shard_map/pallas_call | solution.py:440
  92.0 5.2 %shard_map.91 = (f32[32,128,128]{2,1,0:T(8,128)S(1)}, bf16[64,128,128]{2,1,0:T(8,128)(2,1)S(1)}) custom-call(s32[120]{0:T(128)S(1)} %copy-done.5, s32[120]{0:T(128)S(1)} %bitcast.16, bf16[128,4096]{1,0:T(8,128)(2,1)S(1)} %shard_map.90.hidden_ref, f32[32,1,128]{2,1,0:T(1,128)S(1)} %get-tuple-element.24.deg_ref, ...), custom_call_target="tpu_custom_call" | custom-call | tf_op jit(solution)/shard_map/pallas_call | solution.py:463
  97.2 66.3 %shard_map.92 = (bf16[64,128,128]{2,1,0:T(8,128)(2,1)S(1)}, bf16[128,4096]{1,0:T(8,128)(2,1)S(1)}, f32[8,16,512]{2,1,0:T(8,128)S(1)}) custom-call(bf16[64,128,128]{2,1,0:T(8,128)(2,1)S(1)} %get-tuple-element.26.terms_ref, bf16[512,1024]{1,0:T(8,128)(2,1)S(1)} %get-tuple-element.31.rows_ref, bf16[4,8,16,512]{3,2,1,0:T(8,128)(2,1)S(1)} %bitcast.11), custom_call_target="tpu_custom_call" | custom-call | tf_op jit(solution)/shard_map/pallas_call | solution.py:490
  163.5 2.6 %shard_map.93 = bf16[128,4096]{1,0:T(8,128)(2,1)} custom-call(s32[8,128]{1,0:T(8,128)S(1)} %bitcast.14, f32[32,128,128]{2,1,0:T(8,128)S(1)} %get-tuple-element.28.own_ref, bf16[64,128,128]{2,1,0:T(8,128)(2,1)S(1)} %get-tuple-element.29.back_ref), custom_call_target="tpu_custom_call" | custom-call | tf_op jit(solution)/shard_map/pallas_call | solution.py:510
  166.1 1.0 copy.11
  167.1 0.7 copy.12
Async XLA Ops:
  0.6 0.7 copy-start.6
  9.0 1.2 copy-start
  10.2 1.6 copy-start.1
  10.2 1.7 copy-start.3
  10.2 1.7 copy-start.4
  11.9 38.3 %copy-start.5 = (s32[120]{0:T(128)S(1)}, s32[120]{0:T(128)}, u32[]{:S(2)}) copy-start(s32[120]{0:T(128)} %rows_ref.3) | copy-start | bytes 1444
  50.2 2.1 %copy-start.2 = (bf16[120,128,128]{2,1,0:T(8,128)(2,1)S(1)}, bf16[120,128,128]{2,1,0:T(8,128)(2,1)}, u32[]{:S(2)}) copy-start(bf16[120,128,128]{2,1,0:T(8,128)(2,1)} %get-tuple-element.22.turned_ref) | copy-start | bytes 11796484

commit v4 on v3

--- a/solution.py
+++ b/solution.py
@@ -226,30 +226,76 @@
     return pl.ds(pl.multiple_of(index * size, size), size)
 
 
-def swap_kernel(feats, to_columns, src_ref, dst_ref, send_sem, recv_sem, self_sem):
+def dense_kernel(
+    feats, parts, agg_ref, cot_ref, weight_ref, hidden_ref, activ_ref, part_ref,
+    nodes, grads, outgoing, turned, in_send, in_recv, out_send, out_recv, self_sem,
+):
     node, feat = lax.axis_index("node"), lax.axis_index("feat")
+    depth = agg_ref.shape[0]
+    per_feat = nodes.shape[1]
+    width = per_feat // parts
     barrier(0, feats)
-    depth = min(src_ref.shape[0], dst_ref.shape[0])
-    width = min(src_ref.shape[1], dst_ref.shape[1])
-
-    def ends(peer):
-        if to_columns:
-            return src_ref.at[band(peer, depth)], dst_ref.at[:, band(feat, width)]
-        return src_ref.at[:, band(peer, width)], dst_ref.at[band(feat, depth)]
-
-    copies = []
-    for off in range(1, feats):
-        peer = lax.rem(feat + off, feats)
-        src, dst = ends(peer)
-        copies.append(pltpu.make_async_remote_copy(
-            src_ref=src, dst_ref=dst, send_sem=send_sem.at[off - 1],
-            recv_sem=recv_sem.at[off - 1], device_id=(node, peer), device_id_type=MESH,
-        ))
-    src, dst = ends(feat)
-    copies.append(pltpu.make_async_copy(src, dst, self_sem))
-    for copy in copies:
-        copy.start()
-    for copy in copies:
+    arrivals, selfs = [], []
+    for c in range(parts):
+        here = pl.ds(c * width, width)
+        arrivals.append([])
+        for off in range(1, feats):
+            peer = lax.rem(feat + off, feats)
+            columns = pl.ds(pl.multiple_of(peer * per_feat + c * width, width), width)
+            arrivals[c].append(pltpu.make_async_remote_copy(
+                src_ref=agg_ref.at[:, columns], dst_ref=nodes.at[band(feat, depth), here],
+                send_sem=in_send.at[c, off - 1], recv_sem=in_recv.at[c, off - 1],
+                device_id=(node, peer), device_id_type=MESH,
+            ))
+        columns = pl.ds(pl.multiple_of(feat * per_feat + c * width, width), width)
+        selfs.append(pltpu.make_async_copy(
+            agg_ref.at[:, columns], nodes.at[band(feat, depth), here], self_sem.at[c]
+        ))
+    for c in range(parts):
+        for copy in arrivals[c] + [selfs[c]]:
+            copy.start()
+    turned[...] = weight_ref[...].astype(jnp.float32).T.astype(jnp.bfloat16)
+    returns = []
+    for c in range(parts):
+        for copy in arrivals[c] + [selfs[c]]:
+            copy.wait()
+
+        @pl.loop(0, width // LANES)
+        def _(i):
+            columns = pl.ds(pl.multiple_of(c * width + i * LANES, LANES), LANES)
+            preact = jnp.dot(turned[...], nodes[:, columns], preferred_element_type=jnp.float32)
+            sig = jax.nn.sigmoid(preact)
+            activ_ref[:, columns] = (preact * sig).astype(jnp.bfloat16)
+            slope = sig * (1.0 + preact * (1.0 - sig))
+            grad = (cot_ref[:, columns].astype(jnp.float32) * slope).astype(jnp.bfloat16)
+            grads[:, columns] = grad
+            outgoing[:, columns] = jnp.dot(
+                weight_ref[...], grad, preferred_element_type=jnp.float32
+            ).astype(jnp.bfloat16)
+
+        here = pl.ds(c * width, width)
+        columns = pl.ds(pl.multiple_of(feat * per_feat + c * width, width), width)
+        for off in range(1, feats):
+            peer = lax.rem(feat + off, feats)
+            returns.append(pltpu.make_async_remote_copy(
+                src_ref=outgoing.at[band(peer, depth), here], dst_ref=hidden_ref.at[:, columns],
+                send_sem=out_send.at[c, off - 1], recv_sem=out_recv.at[c, off - 1],
+                device_id=(node, peer), device_id_type=MESH,
+            ))
+            returns[-1].start()
+        returns.append(pltpu.make_async_copy(
+            outgoing.at[band(feat, depth), here], hidden_ref.at[:, columns], self_sem.at[parts + c]
+        ))
+        returns[-1].start()
+
+    @pl.loop(0, part_ref.shape[0] // LANES)
+    def _(i):
+        rows = pl.ds(pl.multiple_of(i * LANES, LANES), LANES)
+        part_ref[rows] = lax.dot_general(
+            nodes[rows], grads[...], (((1,), (1,)), ((), ())), preferred_element_type=jnp.float32
+        ).astype(jnp.bfloat16)
+
+    for copy in returns:
         copy.wait()
 
 
@@ -349,11 +395,6 @@
 
     for b in range(blocks):
         out_ref[:, b * LANES : (b + 1) * LANES] = acc[b].astype(jnp.bfloat16)
-
-
-def silu_slope(value):
-    sig = jax.nn.sigmoid(value)
-    return sig * (1.0 + value * (1.0 - sig))
 
 
 def per_device(shards, feats, x_feat, weight, out_grad, tile_rows, tile_cols, tile_masks):
@@ -435,30 +476,26 @@
         compiler_params=params(40),
     )(tile_rows, slot, source, turned)
 
-    def swap(array, to_columns, number):
-        wide = (depth, local_rows) if to_columns else (features, per_feat)
-        return pl.pallas_call(
-            functools.partial(swap_kernel, feats, to_columns),
-            out_shape=shape(wide, bf16),
-            in_specs=[spec(ANY)],
-            out_specs=spec(ANY),
-            scratch_shapes=[dma((feats - 1,)), dma((feats - 1,)), dma(())],
-            compiler_params=params(24, collective_id=number, has_side_effects=True),
-        )(array)
-
-    node_rows = swap(aggregated, False, 3)
-    row_preact = lax.dot_general(
-        full_weight, node_rows, (((0,), (0,)), ((), ())), preferred_element_type=f32
-    )
-    row_activ = jax.nn.silu(row_preact).astype(bf16)
-    grad_rows = (cotangent_rows.astype(f32) * silu_slope(row_preact)).astype(bf16)
-    row_hidden = jnp.dot(full_weight, grad_rows, preferred_element_type=f32).astype(bf16)
-    full_part = lax.dot_general(
-        node_rows, grad_rows, (((1,), (1,)), ((), ())), preferred_element_type=f32
-    )
+    parts = 2 if per_feat % (2 * LANES) == 0 else 1
+    hidden_grad, row_activ, full_part = pl.pallas_call(
+        functools.partial(dense_kernel, feats, parts),
+        out_shape=(
+            shape((depth, local_rows), bf16),
+            shape((hidden, per_feat), bf16),
+            shape((features, hidden), bf16),
+        ),
+        in_specs=[spec(ANY), spec(VMEM), spec(VMEM)],
+        out_specs=(spec(ANY), spec(VMEM), spec(VMEM)),
+        scratch_shapes=[
+            VMEM((features, per_feat), bf16), VMEM((hidden, per_feat), bf16),
+            VMEM((features, per_feat), bf16), VMEM((hidden, features), bf16),
+            dma((parts, feats - 1)), dma((parts, feats - 1)),
+            dma((parts, feats - 1)), dma((parts, feats - 1)), dma((2 * parts,)),
+        ],
+        compiler_params=params(32, collective_id=3, has_side_effects=True),
+    )(aggregated, cotangent_rows, full_weight)
     slice_rows = depth // shards
-    full_part = full_part.astype(bf16).reshape(feats, shards, slice_rows, hidden)
-    hidden_grad = swap(row_hidden, True, 4)
+    full_part = full_part.reshape(feats, shards, slice_rows, hidden)
 
     own, terms = pl.pallas_call(
         functools.partial(spread_kernel, steps, blocks),

time: 168 us -> 163 us (0.970)
  matrix products: 2.92 us -> 0 us
  Pallas kernels: 158 us -> 156 us
    pallas_call x2 -> x1, Pallas kernels: 30.9 us -> 27.6 us  [per_device(): pl.pallas_call(functools.partial(dense_kernel, feats, parts), out_shape=(...]
    dot_general x3 -> x0, matrix products: 2.92 us -> none  [the longest x1 1.44 us: per_device(): lax.dot_general(full_weight, node_rows, (((0,), (0,)), ((), ())), preferr...]
where the time goes in v4:
time: 163 us; the launch traced here: 162 us
  Pallas kernels  156 us (96%)
  local copies, waits for them, and re-layouts  5.66 us (3%)
    pallas_call x1, Pallas kernels, per_device(): pl.pallas_call(functools.partial(return_kernel, shards, feats, (local_row...  67.1 us
    pallas_call x1, Pallas kernels, per_device(): pl.pallas_call(functools.partial(fetch_kernel, shards, feats, blocks), ou...  38.3 us
    pallas_call x1, Pallas kernels, per_device(): pl.pallas_call(functools.partial(dense_kernel, feats, parts), out_shape=(...  27.6 us
    pallas_call x1, Pallas kernels, per_device(): pl.pallas_call(functools.partial(ask_kernel, shards, blocks), out_shape=(...  7.71 us
    pallas_call x1, Pallas kernels, per_device(): pl.pallas_call(functools.partial(gather_kernel, steps, blocks), grid_spec...  5.79 us
    unnamed x16, local copies, waits for them, and re-layouts  5.66 us
    pallas_call x1, Pallas kernels, per_device(): pl.pallas_call(functools.partial(spread_kernel, steps, blocks), grid_spec...  5.21 us

profile of v4, /device:TPU:0, one launch (start us, length us, event | category | flops | bytes accessed | tf_op | source)
XLA Modules:
  0.0 162.3 jit_solution(15078786694985067049)
XLA Ops:
  0.6 0.0 copy-start.6
  0.6 0.6 copy-done.6
  1.3 7.7 %shard_map.85 = (s32[8,1,128]{2,1,0:T(1,128)S(1)}, s32[1,120]{1,0:T(1,128)S(1)}) custom-call(s32[1,120]{1,0:T(1,128)S(1)} %bitcast.11), custom_call_target="tpu_custom_call" | custom-call | tf_op jit(solution)/shard_map/pallas_call | solution.py:413
  9.0 0.0 copy-start
  9.0 1.2 copy-done
  10.2 0.0 copy-start.1
  10.2 0.0 copy-start.3
  10.2 0.0 copy-start.4
  10.2 1.6 %shard_map.86.outbox_ref = bf16[64,128,128]{2,1,0:T(8,128)(2,1)S(1)} custom-call(s32[8,128]{1,0:T(8,128)S(1)} %bitcast.7, bf16[128,4096]{1,0:T(8,128)(2,1)S(1)} %copy-done), custom_call_target="tpu_custom_call" | custom-call | tf_op jit(solution)/shard_map/pallas_call | solution.py:425
  11.9 0.0 copy-done.1
  11.9 0.0 copy-done.3
  11.9 0.0 copy-done.4
  11.9 0.0 copy-start.5
  11.9 38.3 %shard_map.87 = (bf16[96,128,128]{2,1,0:T(8,128)(2,1)S(1)}, bf16[512,1024]{1,0:T(8,128)(2,1)S(1)}, bf16[512,512]{1,0:T(8,128)(2,1)S(1)}, bf16[120,128,128]{2,1,0:T(8,128)(2,1)S(1)}, bf16[120,128,128]{2,1,0:T(8,128)(2,1)}) custom-call(bf16[64,128,128]{2,1,0:T(8,128)(2,1)S(1)} %shard_map.86.outbox_ref, bf16[128,4096]{1,0:T(8,128)(2,1)S(1)} %copy-done.1, ...), custom_call_target="tpu_custom_call" | custom-call | tf_op jit(solution)/shard_map/pallas_call | solution.py:433
  50.2 0.0 copy-done.5
  50.2 0.0 copy-start.2
  50.2 2.1 %copy-done.2 = bf16[120,128,128]{2,1,0:T(8,128)(2,1)S(1)} copy-done((bf16[120,128,128]{2,1,0:T(8,128)(2,1)S(1)}, bf16[120,128,128]{2,1,0:T(8,128)(2,1)}, u32[]{:S(2)}) %copy-start.2) | copy-done | bytes 3932184
  52.3 5.8 %shard_map.88 = (bf16[128,4096]{1,0:T(8,128)(2,1)S(1)}, f32[32,1,128]{2,1,0:T(1,128)S(1)}) custom-call(s32[120]{0:T(128)S(1)} %copy-done.5, s32[120]{0:T(128)S(1)} %bitcast.9, bf16[96,128,128]{2,1,0:T(8,128)(2,1)S(1)} %get-tuple-element.22.source_ref, bf16[120,128,128]{2,1,0:T(8,128)(2,1)S(1)} %copy-done.2), custom_call_target="tpu_custom_call" | custom-call | tf_op jit(solution)/shard_map/pallas_call | solution.py:457
  58.1 27.6 %shard_map.89 = (bf16[128,4096]{1,0:T(8,128)(2,1)S(1)}, bf16[512,1024]{1,0:T(8,128)(2,1)S(1)}, bf16[512,512]{1,0:T(8,128)(2,1)S(1)}) custom-call(bf16[128,4096]{1,0:T(8,128)(2,1)S(1)} %get-tuple-element.24.agg_ref, bf16[512,1024]{1,0:T(8,128)(2,1)S(1)} %get-tuple-element.25.cot_ref, bf16[512,512]{1,0:T(8,128)(2,1)S(1)} %get-tuple-element.26.weight_ref), custom_call_target="tpu_custom_call" | custom-call | tf_op jit(solution)/shard_map/pallas_call | solution.py:480
  85.7 5.2 %shard_map.90 = (f32[32,128,128]{2,1,0:T(8,128)S(1)}, bf16[64,128,128]{2,1,0:T(8,128)(2,1)S(1)}) custom-call(s32[120]{0:T(128)S(1)} %copy-done.5, s32[120]{0:T(128)S(1)} %bitcast.10, bf16[128,4096]{1,0:T(8,128)(2,1)S(1)} %get-tuple-element.27.hidden_ref, f32[32,1,128]{2,1,0:T(1,128)S(1)} %get-tuple-element.28.deg_ref, ...), custom_call_target="tpu_custom_call" | custom-call | tf_op jit(solution)/shard_map/pallas_call | solution.py:500
  90.9 67.1 %shard_map.91 = (bf16[64,128,128]{2,1,0:T(8,128)(2,1)S(1)}, bf16[128,4096]{1,0:T(8,128)(2,1)S(1)}, f32[8,16,512]{2,1,0:T(8,128)S(1)}) custom-call(bf16[64,128,128]{2,1,0:T(8,128)(2,1)S(1)} %get-tuple-element.30.terms_ref, bf16[512,1024]{1,0:T(8,128)(2,1)S(1)} %get-tuple-element.31.rows_ref, bf16[4,8,16,512]{3,2,1,0:T(8,128)(2,1)S(1)} %bitcast.5), custom_call_target="tpu_custom_call" | custom-call | tf_op jit(solution)/shard_map/pallas_call | solution.py:527
  158.0 2.6 %shard_map.92 = bf16[128,4096]{1,0:T(8,128)(2,1)} custom-call(s32[8,128]{1,0:T(8,128)S(1)} %bitcast.8, f32[32,128,128]{2,1,0:T(8,128)S(1)} %get-tuple-element.34.own_ref, bf16[64,128,128]{2,1,0:T(8,128)(2,1)S(1)} %get-tuple-element.35.back_ref), custom_call_target="tpu_custom_call" | custom-call | tf_op jit(solution)/shard_map/pallas_call | solution.py:547
  160.6 1.0 copy.11
  161.6 0.7 copy.12
Async XLA Ops:
  0.6 0.7 copy-start.6
  9.0 1.2 copy-start
  10.2 1.6 %copy-start.1 = (bf16[128,4096]{1,0:T(8,128)(2,1)S(1)}, bf16[128,4096]{1,0:T(8,128)(2,1)}, u32[]{:S(2)}) copy-start(bf16[128,4096]{1,0:T(8,128)(2,1)} %x_ref.3) | copy-start | bytes 3145732
  10.2 1.7 %copy-start.3 = (bf16[128,4096]{1,0:T(8,128)(2,1)S(1)}, bf16[128,4096]{1,0:T(8,128)(2,1)}, u32[]{:S(2)}) copy-start(bf16[128,4096]{1,0:T(8,128)(2,1)} %grad_ref.1) | copy-start | bytes 3145732
  10.2 1.7 %copy-start.4 = (bf16[128,512]{1,0:T(8,128)(2,1)S(1)}, bf16[128,512]{1,0:T(8,128)(2,1)}, u32[]{:S(2)}) copy-start(bf16[128,512]{1,0:T(8,128)(2,1)} %weight_ref.1) | copy-start | bytes 393220
  11.9 38.3 %copy-start.5 = (s32[120]{0:T(128)S(1)}, s32[120]{0:T(128)}, u32[]{:S(2)}) copy-start(s32[120]{0:T(128)} %rows_ref.3) | copy-start | bytes 1444
  50.2 2.1 %copy-start.2 = (bf16[120,128,128]{2,1,0:T(8,128)(2,1)S(1)}, bf16[120,128,128]{2,1,0:T(8,128)(2,1)}, u32[]{:S(2)}) copy-start(bf16[120,128,128]{2,1,0:T(8,128)(2,1)} %get-tuple-element.23.turned_ref) | copy-start | bytes 11796484

commit v5 on v4

--- a/solution.py
+++ b/solution.py
@@ -418,7 +418,7 @@
         scratch_shapes=[
             VMEM((shards, 1, LANES), i32), dma((shards - 1,)), dma((shards - 1,)), dma(()),
         ],
-        compiler_params=params(16, collective_id=2, has_side_effects=True),
+        compiler_params=params(8, collective_id=2, has_side_effects=True),
     )(tile_cols.reshape(1, tiles))
     asked, slot = asked.reshape(shards, LANES), slot.reshape(tiles)
 
@@ -427,7 +427,7 @@
         out_shape=shape((shards * CAP, depth, LANES), bf16),
         in_specs=[spec(SMEM), spec(VMEM)],
         out_specs=spec(VMEM),
-        compiler_params=params(24),
+        compiler_params=params(10),
     )(asked, x_feat)
 
     source, cotangent_rows, full_weight, edges, turned = pl.pallas_call(
@@ -448,7 +448,7 @@
             dma((feats - 1,)), dma((feats - 1,)), dma((feats - 1,)), dma((feats - 1,)),
             dma((3,)),
         ],
-        compiler_params=params(40, collective_id=0, has_side_effects=True),
+        compiler_params=params(tiles // 8 + 5, collective_id=0, has_side_effects=True),
     )(outbox, x_feat, out_grad, weight, tile_masks)
 
     whole3 = lambda i, *_: (0, 0, 0)
@@ -473,7 +473,7 @@
             shape((depth, local_rows), bf16),
             shape((blocks, 1, LANES), f32),
         ),
-        compiler_params=params(40),
+        compiler_params=params(16),
     )(tile_rows, slot, source, turned)
 
     parts = 2 if per_feat % (2 * LANES) == 0 else 1
@@ -492,7 +492,7 @@
             dma((parts, feats - 1)), dma((parts, feats - 1)),
             dma((parts, feats - 1)), dma((parts, feats - 1)), dma((2 * parts,)),
         ],
-        compiler_params=params(32, collective_id=3, has_side_effects=True),
+        compiler_params=params(16, collective_id=3, has_side_effects=True),
     )(aggregated, cotangent_rows, full_weight)
     slice_rows = depth // shards
     full_part = full_part.reshape(feats, shards, slice_rows, hidden)
@@ -520,7 +520,7 @@
             shape((blocks, depth, LANES), f32),
             shape((shards * CAP, depth, LANES), bf16),
         ),
-        compiler_params=params(40),
+        compiler_params=params(24),
     )(tile_rows, slot, hidden_grad, degree, edges)
 
     piece = (slice_rows, hidden)
@@ -540,7 +540,7 @@
             dma((feats - 1,)), dma((feats - 1,)), dma((shards - 1,)), dma((shards - 1,)),
             dma((shards - 1,)), dma((shards - 1,)),
         ],
-        compiler_params=params(24, collective_id=1, has_side_effects=True),
+        compiler_params=params(8, collective_id=1, has_side_effects=True),
     )(terms, row_activ, full_part)
     weight_grad = weight_grad.reshape(depth, hidden)
 

time: 163 us -> 164 us (level)
  no operation moved by 1% of the time
where the time goes in v5:
time: 164 us; the launch traced here: 163 us
  Pallas kernels  156 us (95%)
  local copies, waits for them, and re-layouts  6.78 us (4%)
    pallas_call x1, Pallas kernels, per_device(): pl.pallas_call(functools.partial(return_kernel, shards, feats, (local_row...  67 us
    pallas_call x1, Pallas kernels, per_device(): pl.pallas_call(functools.partial(fetch_kernel, shards, feats, blocks), ou...  38.7 us
    pallas_call x1, Pallas kernels, per_device(): pl.pallas_call(functools.partial(dense_kernel, feats, parts), out_shape=(...  27.6 us
    pallas_call x1, Pallas kernels, per_device(): pl.pallas_call(functools.partial(ask_kernel, shards, blocks), out_shape=(...  7.71 us
    unnamed x16, local copies, waits for them, and re-layouts  6.78 us
    pallas_call x1, Pallas kernels, per_device(): pl.pallas_call(functools.partial(gather_kernel, steps, blocks), grid_spec...  5.74 us
    pallas_call x1, Pallas kernels, per_device(): pl.pallas_call(functools.partial(spread_kernel, steps, blocks), grid_spec...  4.99 us

profile of v5, /device:TPU:0, one launch (start us, length us, event | category | flops | bytes accessed | tf_op | source)
XLA Modules:
  0.0 163.5 jit_solution(2642448504111990199)
XLA Ops:
  0.6 0.0 copy-start.6
  0.6 0.6 copy-done.6
  1.3 7.7 %shard_map.85 = (s32[8,1,128]{2,1,0:T(1,128)S(1)}, s32[1,120]{1,0:T(1,128)S(1)}) custom-call(s32[1,120]{1,0:T(1,128)S(1)} %bitcast.11), custom_call_target="tpu_custom_call" | custom-call | tf_op jit(solution)/shard_map/pallas_call | solution.py:413
  9.0 0.0 copy-start.1
  9.0 1.2 copy-done.1
  10.2 0.0 copy-start.2
  10.2 0.0 copy-start.3
  10.2 0.0 copy-start.4
  10.2 1.6 shard_map.86.outbox_ref
  11.9 0.0 copy-done.2
  11.9 0.0 copy-done.3
  11.9 0.0 copy-done.4
  11.9 0.0 copy-start
  11.9 3.2 %copy-done = s32[120,128,128]{2,1,0:T(8,128)S(1)} copy-done((s32[120,128,128]{2,1,0:T(8,128)S(1)}, s32[120,128,128]{2,1,0:T(8,128)}, u32[]{:S(2)}) %copy-start) | copy-done | bytes 7864344
  15.1 0.0 copy-start.5
  15.1 38.7 %shard_map.87 = (bf16[96,128,128]{2,1,0:T(8,128)(2,1)S(1)}, bf16[512,1024]{1,0:T(8,128)(2,1)S(1)}, bf16[512,512]{1,0:T(8,128)(2,1)S(1)}, bf16[120,128,128]{2,1,0:T(8,128)(2,1)S(1)}, bf16[120,128,128]{2,1,0:T(8,128)(2,1)S(1)}) custom-call(bf16[64,128,128]{2,1,0:T(8,128)(2,1)S(1)} %shard_map.86.outbox_ref, bf16[128,4096]{1,0:T(8,128)(2,1)S(1)} %copy-done.2, ...), custom_call_target="tpu_custom_call" | custom-call | tf_op jit(solution)/shard_map/pallas_call | solution.py:433
  53.9 0.0 copy-done.5
  53.9 5.7 %shard_map.88 = (bf16[128,4096]{1,0:T(8,128)(2,1)S(1)}, f32[32,1,128]{2,1,0:T(1,128)S(1)}) custom-call(s32[120]{0:T(128)S(1)} %copy-done.5, s32[120]{0:T(128)S(1)} %bitcast.9, bf16[96,128,128]{2,1,0:T(8,128)(2,1)S(1)} %get-tuple-element.22.source_ref, bf16[120,128,128]{2,1,0:T(8,128)(2,1)S(1)} %get-tuple-element.23.turned_ref), custom_call_target="tpu_custom_call" | custom-call | tf_op jit(solution)/shard_map/pallas_call | solution.py:457
  59.6 27.6 %shard_map.89 = (bf16[128,4096]{1,0:T(8,128)(2,1)S(1)}, bf16[512,1024]{1,0:T(8,128)(2,1)S(1)}, bf16[512,512]{1,0:T(8,128)(2,1)S(1)}) custom-call(bf16[128,4096]{1,0:T(8,128)(2,1)S(1)} %get-tuple-element.24.agg_ref, bf16[512,1024]{1,0:T(8,128)(2,1)S(1)} %get-tuple-element.25.cot_ref, bf16[512,512]{1,0:T(8,128)(2,1)S(1)} %get-tuple-element.26.weight_ref), custom_call_target="tpu_custom_call" | custom-call | tf_op jit(solution)/shard_map/pallas_call | solution.py:480
  87.2 5.0 %shard_map.90 = (f32[32,128,128]{2,1,0:T(8,128)S(1)}, bf16[64,128,128]{2,1,0:T(8,128)(2,1)S(1)}) custom-call(s32[120]{0:T(128)S(1)} %copy-done.5, s32[120]{0:T(128)S(1)} %bitcast.10, bf16[128,4096]{1,0:T(8,128)(2,1)S(1)} %get-tuple-element.27.hidden_ref, f32[32,1,128]{2,1,0:T(1,128)S(1)} %get-tuple-element.28.deg_ref, ...), custom_call_target="tpu_custom_call" | custom-call | tf_op jit(solution)/shard_map/pallas_call | solution.py:500
  92.2 67.0 %shard_map.91 = (bf16[64,128,128]{2,1,0:T(8,128)(2,1)S(1)}, bf16[128,4096]{1,0:T(8,128)(2,1)S(1)}, f32[8,16,512]{2,1,0:T(8,128)S(1)}) custom-call(bf16[64,128,128]{2,1,0:T(8,128)(2,1)S(1)} %get-tuple-element.30.terms_ref, bf16[512,1024]{1,0:T(8,128)(2,1)S(1)} %get-tuple-element.31.rows_ref, bf16[4,8,16,512]{3,2,1,0:T(8,128)(2,1)S(1)} %bitcast.5), custom_call_target="tpu_custom_call" | custom-call | tf_op jit(solution)/shard_map/pallas_call | solution.py:527
  159.2 2.6 %shard_map.92 = bf16[128,4096]{1,0:T(8,128)(2,1)} custom-call(s32[8,128]{1,0:T(8,128)S(1)} %bitcast.8, f32[32,128,128]{2,1,0:T(8,128)S(1)} %get-tuple-element.34.own_ref, bf16[64,128,128]{2,1,0:T(8,128)(2,1)S(1)} %get-tuple-element.35.back_ref), custom_call_target="tpu_custom_call" | custom-call | tf_op jit(solution)/shard_map/pallas_call | solution.py:547
  161.8 1.0 copy.11
  162.8 0.7 copy.12
Async XLA Ops:
  0.6 0.7 copy-start.6
  9.0 1.2 copy-start.1
  10.2 1.6 %copy-start.2 = (bf16[128,4096]{1,0:T(8,128)(2,1)S(1)}, bf16[128,4096]{1,0:T(8,128)(2,1)}, u32[]{:S(2)}) copy-start(bf16[128,4096]{1,0:T(8,128)(2,1)} %x_ref.3) | copy-start | bytes 3145732
  10.2 1.7 %copy-start.3 = (bf16[128,4096]{1,0:T(8,128)(2,1)S(1)}, bf16[128,4096]{1,0:T(8,128)(2,1)}, u32[]{:S(2)}) copy-start(bf16[128,4096]{1,0:T(8,128)(2,1)} %grad_ref.1) | copy-start | bytes 3145732
  10.2 1.7 %copy-start.4 = (bf16[128,512]{1,0:T(8,128)(2,1)S(1)}, bf16[128,512]{1,0:T(8,128)(2,1)}, u32[]{:S(2)}) copy-start(bf16[128,512]{1,0:T(8,128)(2,1)} %weight_ref.1) | copy-start | bytes 393220
  11.9 3.2 %copy-start = (s32[120,128,128]{2,1,0:T(8,128)S(1)}, s32[120,128,128]{2,1,0:T(8,128)}, u32[]{:S(2)}) copy-start(s32[120,128,128]{2,1,0:T(8,128)} %mask_ref.1) | copy-start | bytes 23592964
  15.1 38.7 %copy-start.5 = (s32[120]{0:T(128)S(1)}, s32[120]{0:T(128)}, u32[]{:S(2)}) copy-start(s32[120]{0:T(128)} %rows_ref.3) | copy-start | bytes 1444
